TPU v7x, 256 devices: a whole 4x4x8 slice. The times are simulated.
256 devices in a mesh: dp: 4 (over x), mp: 64 (over z, y, core).
Axes of the slice: x: 4, y: 4, z: 8, core: 2. Of those that a mesh axis runs over, the one named last changes fastest.
Arguments:
- partial_grads: bfloat16 [4, 224, 512, 512], P('dp', None, 'mp'), may hold values from -3 to 3
- stat_left: float32 [4, 128, 512, 512], P('dp', 'mp'), as said below
- stat_right: float32 [4, 128, 512, 512], P('dp', 'mp'), as said below
- assign: int32 [224], replicated, may hold values from 0 to 511, as said below
- query_vectors: bfloat16 [1024, 8192], P('dp', 'mp'), may hold values from -36 to 36
- key_vectors: bfloat16 [1024, 8192], P('dp', 'mp'), may hold values from -36 to 36
- value_vectors: bfloat16 [1024, 8192], P('dp', 'mp'), may hold values from -6 to 6
Outputs:
- left_next: float32 [4, 128, 512, 512], P('dp', 'mp')
- right_next: float32 [4, 128, 512, 512], P('dp', 'mp')
- update: bfloat16 [224, 512, 512], P(None, 'mp')
- attended: bfloat16 [1024, 8192], P('dp', 'mp')
Inputs may be any that keep to these rules, and one draw needn't show every extreme that they name: `assign`: distinct values: no slot holds two blocks; in every draw all 2 slots of some device hold blocks. `stat_left`: each slot's matrix is symmetric and positive definite. `stat_right`: each slot's matrix is symmetric and positive definite.
All inputs are finite; a program needn't handle non-finite values.
Results may differ from a plain program's by a relative error of at most 0.014.
Values may be sent and summed in bfloat16 or wider, within the bound.
A program may use at most 128 MiB of HBM per device.

v0:
```python
import math

import jax
import jax.numpy as jnp
from jax import lax
from jax.sharding import PartitionSpec as P

ITERS = 2
HD = 128


BETA = 0.9


def product(left, right):
    return jnp.matmul(left, right, precision=lax.Precision.HIGHEST)


def inverse_root(matrix):
    identity = jnp.eye(matrix.shape[-1], dtype=jnp.float32)
    norm_size = jnp.sqrt(jnp.sum(matrix * matrix, axis=(-2, -1), keepdims=True) + 1e-06)
    scaled = matrix / norm_size
    root = identity
    for iteration in range(ITERS):
        factor = (5.0 * identity - scaled) * 0.25
        if iteration == 0:
            root = factor
        else:
            root = product(root, factor)
        if iteration + 1 < ITERS:
            squared = product(factor, factor)
            scaled = product(product(squared, squared), scaled)
    return root


def precondition(block, left_stat, right_stat):
    widened = block.astype(jnp.float32)
    raw = product(product(inverse_root(left_stat), widened), inverse_root(right_stat))
    ratio = (jnp.mean(widened * widened) + 1e-06) / (jnp.mean(raw * raw) + 1e-06)
    return (raw * jnp.sqrt(ratio)).astype(jnp.bfloat16)


def local_attention(query_vectors, key_vectors, value_vectors):
    length = query_vectors.shape[0]
    local_heads = query_vectors.shape[1] // HD
    shaped = (length, local_heads, HD)
    queries = query_vectors.reshape(shaped)
    keys_local = key_vectors.reshape(shaped)
    values_local = value_vectors.reshape(shaped)
    scale = 1.0 / math.sqrt(HD)
    scores = (
        jnp.einsum("qhd,khd->hqk", queries, keys_local, preferred_element_type=jnp.float32) * scale
    )
    causal = lax.broadcasted_iota(jnp.int32, (length, length), 0) >= lax.broadcasted_iota(
        jnp.int32, (length, length), 1
    )
    scores = jnp.where(causal[None], scores, -jnp.inf)
    highest = jnp.max(scores, axis=-1, keepdims=True)
    weights = jnp.exp(scores - highest)
    probs = (weights / jnp.sum(weights, axis=-1, keepdims=True)).astype(jnp.bfloat16)
    mixed = jnp.einsum("hqk,khd->qhd", probs, values_local, preferred_element_type=jnp.float32)
    return mixed.astype(jnp.bfloat16).reshape(query_vectors.shape)


def body(partial_grads, stat_left, stat_right, assign, query_vectors, key_vectors, value_vectors):
    replica_count = lax.axis_size("dp")
    column_count = lax.axis_size("mp")
    capacity = stat_left.shape[1]
    block_order = partial_grads.shape[3]
    sliver_rows = partial_grads.shape[2]
    total_slots = replica_count * column_count * capacity
    block_count = assign.shape[0]
    source = (
        jnp.full((total_slots,), -1, jnp.int32)
        .at[assign]
        .set(jnp.arange(block_count, dtype=jnp.int32))
    )
    picked = jnp.take(partial_grads[0], jnp.maximum(source, 0), axis=0)
    packed = jnp.where((source >= 0)[:, None, None], picked, jnp.zeros((), jnp.bfloat16))
    grouped = packed.astype(jnp.float32).reshape(
        replica_count, column_count * capacity, sliver_rows, block_order
    )
    summed = lax.psum_scatter(grouped.astype(jnp.bfloat16), "dp", scatter_dimension=0, tiled=True)
    rounded = summed.reshape(column_count, capacity, sliver_rows, block_order)
    owned = lax.all_to_all(rounded, "mp", split_axis=0, concat_axis=2, tiled=True)[0]
    left_gram = jnp.einsum("sik,sjk->sij", owned, owned, preferred_element_type=jnp.float32)
    right_gram = jnp.einsum("ski,skj->sij", owned, owned, preferred_element_type=jnp.float32)
    left_next = BETA * stat_left[0] + (1.0 - BETA) * left_gram
    right_next = BETA * stat_right[0] + (1.0 - BETA) * right_gram
    attended = local_attention(query_vectors, key_vectors, value_vectors)
    updates = jax.vmap(precondition)(owned, left_next, right_next)
    returned = lax.all_to_all(updates, "mp", split_axis=1, concat_axis=0, tiled=True)
    everywhere = lax.all_gather(returned, "dp", axis=0, tiled=True)
    update = jnp.take(everywhere, assign, axis=0)
    return (left_next[None], right_next[None], update, attended)


def solution(mesh):
    placed = (
        P("dp", None, "mp", None),
        P("dp", "mp", None, None),
        P("dp", "mp", None, None),
        P(),
        P("dp", "mp"),
        P("dp", "mp"),
        P("dp", "mp"),
    )
    return jax.shard_map(
        body,
        mesh=mesh,
        in_specs=placed,
        out_specs=(
            P("dp", "mp", None, None),
            P("dp", "mp", None, None),
            P(None, "mp", None),
            P("dp", "mp"),
        ),
        check_vma=False,
    )
```

profile of v0, /device:TPU:2, one launch (start us, length us, event | category | flops | bytes accessed | tf_op | source)
XLA Modules:
  0.0 247.2 jit_solution(17665835253134246278)
XLA Ops:
  7.2 0.0 copy-start
  7.2 0.0 reduce-scatter.2.cloned.1.call-start
  7.2 0.8 compare_select_fusion
  8.0 1.3 scatter_custom_fusion
  9.4 0.0 copy-done
  9.4 3.5 %gather_fusion = bf16[512,8,512]{2,1,0:T(8,128)(2,1)} fusion(bf16[224,8,512]{2,1,0:T(8,128)(2,1)S(1)} %bitcast.55, s32[1024]{0:T(1024)S(1)} %pad_clamp_fusion.1), kind=kCustom, calls=%fused_computation | custom fusion | bytes 8390656 | tf_op jit(solution)/shard_map/jit(_take)/gather | solution.py:78
  12.9 5.3 %select_select_fusion = bf16[4,128,8,512]{3,2,1,0:T(8,128)(2,1)} fusion(bf16[4,128,8,512]{3,2,1,0:T(8,128)(2,1)} %bitcast.56, pred[4,128]{1,0:T(4,128)(4,1)S(1)} %get-tuple-element.5, pred[4,128]{1,0:T(4,128)(4,1)S(1)} %get-tuple-element.4), kind=kLoop, calls=%fused_computation.3 | loop fusion | flops 4194304 | bytes 8389632 | tf_op jit(solution)/shard_map/jit(_where)/select_n | solution.py:79
  18.1 0.0 reduce-scatter.2.cloned.1.call-update
  18.1 51.2 %reduce-scatter.2.cloned.1.call-done = bf16[1,128,8,512]{3,2,1,0:T(8,128)(2,1)} async-done(((bf16[4,128,8,512]{3,2,1,0:T(8,128)(2,1)}), bf16[1,128,8,512]{3,2,1,0:T(8,128)(2,1)}) %reduce-scatter.2.cloned.1.call-update) | async-done | bytes 1048592 | tf_op jit(solution)/shard_map/reduce_scatter | solution.py:83
  69.4 10.5 %all-to-all-start = ((bf16[64,2,8,512]{3,2,1,0:T(8,128)(2,1)}), bf16[64,2,8,512]{3,2,1,0:T(8,128)(2,1)S(1)}, u32[]{:S(2)}, u32[]{:S(2)}) async-start(bf16[64,2,8,512]{3,2,1,0:T(8,128)(2,1)} %bitcast.60), calls=%async_computation.1 | async-start | bytes 2097152 | tf_op jit(solution)/shard_map/all_to_all | solution.py:85
  79.8 0.5 all-gather.2.cloned.1.call-start
  80.3 1.1 fusion.21
  81.4 27.3 %all-to-all-done = bf16[64,2,8,512]{3,2,1,0:T(8,128)(2,1)S(1)} async-done(((bf16[64,2,8,512]{3,2,1,0:T(8,128)(2,1)}), bf16[64,2,8,512]{3,2,1,0:T(8,128)(2,1)S(1)}, u32[]{:S(2)}, u32[]{:S(2)}) %all-to-all-start) | async-done | bytes 1048608 | tf_op jit(solution)/shard_map/all_to_all | solution.py:85
  108.7 2.7 %multiply_reduce_fusion.2 = (f32[2]{0:T(128)S(1)}, f32[2,512,512]{2,1,0:T(8,128)S(1)}) fusion(f32[1,2,512,512]{3,2,1,0:T(8,128)} %param.9, bf16[64,2,8,512]{3,2,1,0:T(8,128)(2,1)S(1)} %all-to-all-done), kind=kOutput, calls=%fused_computation.13 | convolution fusion | flops 539492352 | bytes 5242888 | tf_op jit(solution)/shard_map/ski,skj->sij/dot_general | solution.py:87
  111.5 0.0 copy-done.2
  111.5 4.0 %fusion.7 = f32[2,512,512]{2,1,0:T(8,128)S(1)} fusion(f32[512,512]{1,0:T(8,128)S(1)} %copy-done.2, f32[2,512,512]{2,1,0:T(8,128)S(1)} %get-tuple-element.9, f32[2]{0:T(128)S(1)} %add_sqrt_fusion), kind=kOutput, calls=%fused_computation.20 | convolution fusion | flops 3222798336 | bytes 5242888 | tf_op jit(solution)/shard_map/vmap()/dot_general | solution.py:16
  115.5 3.5 %fusion.37 = f32[2,512,512]{2,1,0:T(8,128)S(1)} fusion(f32[2,512,512]{2,1,0:T(8,128)S(1)} %fusion.7), kind=kOutput, calls=%fused_computation.70 | convolution fusion | flops 3221225472 | bytes 4194304 | tf_op jit(solution)/shard_map/vmap()/dot_general | solution.py:16
  119.0 3.7 %fusion.34 = f32[2,512,512]{2,1,0:T(8,128)S(1)} fusion(f32[2,512,512]{2,1,0:T(8,128)S(1)} %fusion.37, f32[2,512,512]{2,1,0:T(8,128)S(1)} %get-tuple-element.9, f32[2]{0:T(128)S(1)} %add_sqrt_fusion), kind=kOutput, calls=%fused_computation.67 | convolution fusion | flops 3221749760 | bytes 6291464 | tf_op jit(solution)/shard_map/vmap()/dot_general | solution.py:16
  122.8 0.0 copy-done.1
  122.8 0.0 copy-start.6
  122.8 4.0 %fusion = f32[2,512,512]{2,1,0:T(8,128)S(1)} fusion(f32[2,512,512]{2,1,0:T(8,128)S(1)} %fusion.34, f32[512,512]{1,0:T(8,128)S(1)} %copy-done.2, f32[2,512,512]{2,1,0:T(8,128)S(1)} %get-tuple-element.9, f32[2]{0:T(128)S(1)} %add_sqrt_fusion), kind=kOutput, calls=%fused_computation.9 | convolution fusion | flops 3223846912 | bytes 7340040 | tf_op jit(solution)/shard_map/vmap()/dot_general | solution.py:16
  126.8 1.1 multiply_reduce_fusion.3
  127.9 4.0 %fusion.6 = f32[2,512,512]{2,1,0:T(8,128)S(1)} fusion(f32[512,512]{1,0:T(8,128)S(1)} %copy-done.2, f32[2,512,512]{2,1,0:T(8,128)S(1)} %get-tuple-element.7, f32[2]{0:T(128)S(1)} %add_sqrt_fusion.1), kind=kOutput, calls=%fused_computation.19 | convolution fusion | flops 3222798336 | bytes 5242888 | tf_op jit(solution)/shard_map/vmap()/dot_general | solution.py:16
  131.9 3.5 %fusion.36 = f32[2,512,512]{2,1,0:T(8,128)S(1)} fusion(f32[2,512,512]{2,1,0:T(8,128)S(1)} %fusion.6), kind=kOutput, calls=%fused_computation.69 | convolution fusion | flops 3221225472 | bytes 4194304 | tf_op jit(solution)/shard_map/vmap()/dot_general | solution.py:16
  135.5 3.9 %fusion.33 = f32[2,512,512]{2,1,0:T(8,128)S(1)} fusion(f32[2,512,512]{2,1,0:T(8,128)S(1)} %fusion.36, f32[2,512,512]{2,1,0:T(8,128)S(1)} %get-tuple-element.7, f32[2]{0:T(128)S(1)} %add_sqrt_fusion.1), kind=kOutput, calls=%fused_computation.66 | convolution fusion | flops 3221749760 | bytes 6291464 | tf_op jit(solution)/shard_map/vmap()/dot_general | solution.py:16
  139.4 0.0 copy-done.8
  139.4 3.8 %fusion.3 = f32[2,512,512]{2,1,0:T(8,128)S(1)} fusion(f32[2,512,512]{2,1,0:T(8,128)S(1)} %fusion.33, f32[512,512]{1,0:T(8,128)S(1)} %copy-done.2, f32[2,512,512]{2,1,0:T(8,128)S(1)} %get-tuple-element.7, f32[2]{0:T(128)S(1)} %add_sqrt_fusion.1), kind=kOutput, calls=%fused_computation.14 | convolution fusion | flops 3223846912 | bytes 7340040 | tf_op jit(solution)/shard_map/vmap()/dot_general | solution.py:16
  143.2 1.8 fusion.9
  145.0 3.8 %multiply_reduce_fusion = (f32[2]{0:T(128)S(1)}, f32[2,512,512]{2,1,0:T(8,128)S(1)}) fusion(f32[2,512,512]{2,1,0:T(8,128)S(1)} %fusion.9, f32[2,512,512]{2,1,0:T(8,128)S(1)} %fusion), kind=kOutput, calls=%fused_computation.7 | convolution fusion | flops 3222274048 | bytes 6291464 | tf_op jit(solution)/shard_map/vmap()/dot_general | solution.py:16
  148.8 0.4 multiply_reduce_fusion.1
  149.2 0.3 multiply_convert_fusion
  149.6 1.1 copy.20
  150.6 34.3 %all_to_all.33 = bf16[2,512,512]{2,0,1:T(2,128)(2,1)S(1)} all-to-all(bf16[2,512,512]{2,0,1:T(2,128)(2,1)S(1)} %copy.20), channel_id=1, replica_groups=mesh['dp'=4,'mp'=64] {'mp'}, dimensions={1} | all-to-all | bytes 2097152 | tf_op jit(solution)/shard_map/all_to_all | solution.py:92
  184.9 0.2 copy.41
  185.1 0.0 copy-start.3
  185.1 0.0 copy-start.4
  185.1 0.0 copy-start.5
  185.1 0.0 copy-start.7
  185.1 1.1 copy.22
  186.2 0.0 all-gather.2.cloned.1.call-update
  186.3 0.2 fusion.35
  186.5 0.1 fusion.25
  186.6 0.0 copy-done.5
  186.6 0.0 copy-done.7
  186.6 0.9 convolution_convert_fusion
  187.5 45.2 %all-gather.2.cloned.1.call-done = bf16[512,8,512]{2,1,0:T(8,128)(2,1)} async-done(((bf16[128,8,512]{2,1,0:T(8,128)(2,1)}), bf16[512,8,512]{2,1,0:T(8,128)(2,1)}) %all-gather.2.cloned.1.call-update) | async-done | bytes 4194320 | tf_op jit(solution)/shard_map/all_gather | solution.py:93
  232.7 4.4 %gather_fusion.1 = bf16[224,8,512]{2,1,0:T(8,128)(2,1)} fusion(bf16[512,8,512]{2,1,0:T(8,128)(2,1)} %all-gather.2.cloned.1.call-done, s32[1024]{0:T(1024)S(1)} %pad_clamp_fusion), kind=kCustom, calls=%fused_computation.1 | custom fusion | bytes 3670912 | tf_op jit(solution)/shard_map/jit(_take)/gather | solution.py:94
  237.1 3.0 %broadcast_select_fusion = bf16[224,8,512]{2,1,0:T(8,128)(2,1)} fusion(bf16[224,8,512]{2,1,0:T(8,128)(2,1)} %gather_fusion.1, pred[224]{0:T(512)(128)(4,1)S(1)} %compare_and_fusion), kind=kLoop, calls=%fused_computation.21 | loop fusion | flops 917504 | bytes 3670240 | tf_op jit(solution)/shard_map/jit(_take)/select_n | solution.py:94
  (15 shorter events, 0.1 us)
Async XLA Ops:
  7.2 2.2 copy-start
  7.2 62.2 %reduce-scatter.2.cloned.1.call-start = ((), (), s32[]{:S(2)}) async-start(), calls=%async_computation.3 | async-start | bytes 5242880 | tf_op jit(solution)/shard_map/reduce_scatter | solution.py:83
  69.4 39.4 %all-to-all-start = ((bf16[64,2,8,512]{3,2,1,0:T(8,128)(2,1)}), bf16[64,2,8,512]{3,2,1,0:T(8,128)(2,1)S(1)}, u32[]{:S(2)}, u32[]{:S(2)}) async-start(bf16[64,2,8,512]{3,2,1,0:T(8,128)(2,1)} %bitcast.60), calls=%async_computation.1 | async-start | bytes 2097152 | tf_op jit(solution)/shard_map/all_to_all | solution.py:85
  79.8 152.8 %all-gather.2.cloned.1.call-start = ((), (), s32[]{:S(2)}) async-start(), calls=%async_computation.4 | async-start | bytes 5242880 | tf_op jit(solution)/shard_map/all_gather | solution.py:93
  108.7 2.8 %copy-start.2 = (f32[512,512]{1,0:T(8,128)S(1)}, f32[512,512]{1,0:T(8,128)}, u32[]{:S(2)}) copy-start(f32[512,512]{1,0:T(8,128)} %fusion.21) | copy-start | bytes 3145732
  111.5 11.3 %copy-start.1 = (f32[2,512,512]{2,1,0:T(8,128)}, f32[2,512,512]{2,1,0:T(8,128)S(1)}, u32[]{:S(2)}) copy-start(f32[2,512,512]{2,1,0:T(8,128)S(1)} %get-tuple-element.9) | copy-start | bytes 6291460
  122.8 4.0 %copy-start.6 = (f32[1,2,512,512]{3,2,1,0:T(8,128)S(1)}, f32[1,2,512,512]{3,2,1,0:T(8,128)}, u32[]{:S(2)}) copy-start(f32[1,2,512,512]{3,2,1,0:T(8,128)} %param.8) | copy-start | bytes 6291460
  127.9 11.5 %copy-start.8 = (f32[2,512,512]{2,1,0:T(8,128)}, f32[2,512,512]{2,1,0:T(8,128)S(1)}, u32[]{:S(2)}) copy-start(f32[2,512,512]{2,1,0:T(8,128)S(1)} %get-tuple-element.7) | copy-start | bytes 6291460
  185.1 1.2 copy-start.3
  185.1 1.2 copy-start.4
  185.1 1.5 copy-start.5
  185.1 1.5 copy-start.7
Sparse Core Ops, SparseCore 0:
  18.3 51.0 reduce-scatter.1
  186.4 46.2 all-gather.1
where the time goes:
time: 252 us; the launch traced here: 247 us
  waiting for transfers between devices  124 us (49%)
  matrix products  41 us (16%)
  blocking collectives  34.3 us (14%)
  between operations  14.5 us (6%)
  local copies, waits for them, and re-layouts  11.6 us (5%)
  other arithmetic  11.1 us (4%)
  starting transfers between devices  11 us (4%)
    reduce_scatter x1, waiting for transfers between devices, body(): lax.psum_scatter(grouped.astype(jnp.bfloat16), 'dp', scatter_dimension=0,...  51.2 us
    all_gather x1, waiting for transfers between devices, body(): everywhere = lax.all_gather(returned, 'dp', axis=0, tiled=True)  45.2 us
    dot_general x10, matrix products, product(): return jnp.matmul(left, right, precision=lax.Precision.HIGHEST)  36.1 us
    all_to_all x1, blocking collectives, body(): lax.all_to_all(updates, 'mp', split_axis=1, concat_axis=0, tiled=True)  34.3 us
    all_to_all x1, waiting for transfers between devices, body(): lax.all_to_all(rounded, 'mp', split_axis=0, concat_axis=2, tiled=True)[0]  27.3 us
    all_to_all x1, starting transfers between devices, body(): lax.all_to_all(rounded, 'mp', split_axis=0, concat_axis=2, tiled=True)[0]  10.5 us
    select_n x1, other arithmetic, body(): jnp.where((source >= 0)[:, None, None], picked, jnp.zeros((), jnp.bfloat16))  5.25 us
  transfers between devices with their start and end apart: 3, of which 3 were waited for; matrix products, arithmetic and copies ran while one was open for 1% of the time, Pallas kernels for 0%

commit v1 on v0

--- a/solution.py
+++ b/solution.py
@@ -5,37 +5,36 @@
 from jax import lax
 from jax.sharding import PartitionSpec as P
 
-ITERS = 2
 HD = 128
 
 
 BETA = 0.9
 
 
-def product(left, right):
-    return jnp.matmul(left, right, precision=lax.Precision.HIGHEST)
+def narrow(left, right):
+    return jnp.matmul(
+        left.astype(jnp.bfloat16), right.astype(jnp.bfloat16), preferred_element_type=jnp.float32
+    )
 
 
-def inverse_root(matrix):
-    identity = jnp.eye(matrix.shape[-1], dtype=jnp.float32)
+def root_excess(matrix):
     norm_size = jnp.sqrt(jnp.sum(matrix * matrix, axis=(-2, -1), keepdims=True) + 1e-06)
-    scaled = matrix / norm_size
-    root = identity
-    for iteration in range(ITERS):
-        factor = (5.0 * identity - scaled) * 0.25
-        if iteration == 0:
-            root = factor
-        else:
-            root = product(root, factor)
-        if iteration + 1 < ITERS:
-            squared = product(factor, factor)
-            scaled = product(product(squared, squared), scaled)
-    return root
+    first = matrix / norm_size
+    second = narrow(first, first)
+    third = narrow(second, first)
+    tail = (250.0 * first - 25.0 * second + third) * (1.0 / 4096.0)
+    return (
+        -(5.0 / 16.0 + 3125.0 / 4096.0) * first
+        + (3125.0 / 4096.0) * second
+        - (1250.0 / 4096.0) * third
+        + narrow(tail, third)
+    )
 
 
 def precondition(block, left_stat, right_stat):
     widened = block.astype(jnp.float32)
-    raw = product(product(inverse_root(left_stat), widened), inverse_root(right_stat))
+    half = (25.0 / 16.0) * widened + narrow(root_excess(left_stat), block)
+    raw = (25.0 / 16.0) * half + narrow(half, root_excess(right_stat))
     ratio = (jnp.mean(widened * widened) + 1e-06) / (jnp.mean(raw * raw) + 1e-06)
     return (raw * jnp.sqrt(ratio)).astype(jnp.bfloat16)
 

time: 252 us -> 240 us (0.952); the launches traced: 247 us -> 238 us
  blocking collectives: 34.3 us -> 73.7 us
  waiting for transfers between devices: 124 us -> 96.4 us
  matrix products: 41 us -> 27.1 us
  starting transfers between devices: 11 us -> 0.08 us
  local copies, waits for them, and re-layouts: 11.6 us -> 15.3 us
    all_to_all x0 -> x1, blocking collectives: none -> 39.5 us  [body(): lax.all_to_all(rounded, 'mp', split_axis=0, concat_axis=2, tiled=True)[0]]
    all_to_all x1 -> x0, waiting for transfers between devices: 27.3 us -> none  [body(): lax.all_to_all(rounded, 'mp', split_axis=0, concat_axis=2, tiled=True)[0]]
    dot_general x10 -> x6, matrix products: 36.1 us -> 23.8 us  [narrow(): jnp.matmul(left.astype(jnp.bfloat16), right.astype(jnp.bfloat16), preferr...]
    all_to_all x1 -> x0, starting transfers between devices: 10.5 us -> none  [body(): lax.all_to_all(rounded, 'mp', split_axis=0, concat_axis=2, tiled=True)[0]]
    unnamed x18 -> x22, local copies, waits for them, and re-layouts: 0.05 us -> 3.74 us
  transfers between devices with their start and end apart: 3 -> 2, of which waited for: 3 -> 2; matrix products, arithmetic and copies ran while one was open for 1% -> 0% of each run, Pallas kernels for 0% -> 0%
where the time goes in v1:
time: 240 us; the launch traced here: 238 us
  waiting for transfers between devices  96.4 us (40%)
  blocking collectives  73.7 us (31%)
  matrix products  27.1 us (11%)
  local copies, waits for them, and re-layouts  15.3 us (6%)
  between operations  14.2 us (6%)
  other arithmetic  11.5 us (5%)
    reduce_scatter x1, waiting for transfers between devices, body(): lax.psum_scatter(grouped.astype(jnp.bfloat16), 'dp', scatter_dimension=0,...  51.2 us
    all_gather x1, waiting for transfers between devices, body(): everywhere = lax.all_gather(returned, 'dp', axis=0, tiled=True)  45.2 us
    all_to_all x1, blocking collectives, body(): lax.all_to_all(rounded, 'mp', split_axis=0, concat_axis=2, tiled=True)[0]  39.5 us
    all_to_all x1, blocking collectives, body(): lax.all_to_all(updates, 'mp', split_axis=1, concat_axis=0, tiled=True)  34.3 us
    dot_general x6, matrix products, narrow(): jnp.matmul(left.astype(jnp.bfloat16), right.astype(jnp.bfloat16), preferr...  23.8 us
    select_n x1, other arithmetic, body(): jnp.where((source >= 0)[:, None, None], picked, jnp.zeros((), jnp.bfloat16))  5.25 us
  transfers between devices with their start and end apart: 2, of which 2 were waited for; matrix products, arithmetic and copies ran while one was open for 0% of the time, Pallas kernels for 0%

profile of v1, /device:TPU:2, one launch (start us, length us, event | category | flops | bytes accessed | tf_op | source)
XLA Modules:
  0.0 238.2 jit_solution(7344313083620464809)
XLA Ops:
  7.2 0.0 copy-start
  7.2 0.0 reduce-scatter.2.cloned.1.call-start
  7.2 0.8 compare_select_fusion
  8.0 1.3 scatter_custom_fusion
  9.4 0.0 copy-done
  9.4 3.5 %gather_fusion = bf16[512,8,512]{2,1,0:T(8,128)(2,1)} fusion(bf16[224,8,512]{2,1,0:T(8,128)(2,1)S(1)} %bitcast.47, s32[1024]{0:T(1024)S(1)} %pad_clamp_fusion.1), kind=kCustom, calls=%fused_computation | custom fusion | bytes 8390656 | tf_op jit(solution)/shard_map/jit(_take)/gather | solution.py:77
  12.9 5.3 %select_select_fusion = bf16[4,128,8,512]{3,2,1,0:T(8,128)(2,1)} fusion(bf16[4,128,8,512]{3,2,1,0:T(8,128)(2,1)} %bitcast.48, pred[4,128]{1,0:T(4,128)(4,1)S(1)} %get-tuple-element.5, pred[4,128]{1,0:T(4,128)(4,1)S(1)} %get-tuple-element.4), kind=kLoop, calls=%fused_computation.3 | loop fusion | flops 4194304 | bytes 8389632 | tf_op jit(solution)/shard_map/jit(_where)/select_n | solution.py:78
  18.1 0.0 reduce-scatter.2.cloned.1.call-update
  18.1 0.0 all-gather.2.cloned.1.call-start
  18.2 51.2 %reduce-scatter.2.cloned.1.call-done = bf16[1,128,8,512]{3,2,1,0:T(8,128)(2,1)} async-done(((bf16[4,128,8,512]{3,2,1,0:T(8,128)(2,1)}), bf16[1,128,8,512]{3,2,1,0:T(8,128)(2,1)}) %reduce-scatter.2.cloned.1.call-update) | async-done | bytes 1048592 | tf_op jit(solution)/shard_map/reduce_scatter | solution.py:82
  69.4 0.0 copy-start.6
  69.4 39.5 %all_to_all.33 = bf16[64,2,8,512]{3,2,1,0:T(8,128)(2,1)S(1)} all-to-all(bf16[64,2,8,512]{3,2,1,0:T(8,128)(2,1)} %bitcast.52), channel_id=1, replica_groups=mesh['dp'=4,'mp'=64] {'mp'}, dimensions={0} | all-to-all | bytes 2097152 | tf_op jit(solution)/shard_map/all_to_all | solution.py:84
  108.8 0.0 copy-done.6
  108.8 1.1 multiply_reduce_fusion.3
  109.9 0.0 copy-start.8
  109.9 0.8 fusion.38
  110.7 0.5 copy-done.8
  111.2 1.4 copy-done.9
  112.6 2.1 fusion.25
  114.8 0.0 copy-done.1
  114.8 1.1 multiply_reduce_fusion.2
  115.9 0.8 fusion.35
  116.7 0.5 copy-done.2
  117.2 1.3 copy-done.10
  118.5 2.1 fusion.6
  120.6 8.3 %multiply_add_fusion.1 = f32[2,512,512]{2,1,0:T(8,128)} fusion(f32[2,512,512]{2,1,0:T(8,128)} %fusion.25, f32[2,512,512]{2,1,0:T(8,128)} %copy-done.9, f32[2,512,512]{2,1,0:T(8,128)} %copy-done.8, f32[2]{0:T(128)S(1)} %add_sqrt_fusion.1, bf16[64,2,8,512]{3,2,1,0:T(8,128)(2,1)S(1)} %all_to_all.33), kind=kOutput, calls=%fused_computation.16 | convolution fusion | flops 1083703296 | bytes 9437192 | tf_op jit(solution)/shard_map/vmap()/dot_general | solution.py:15
  128.9 9.6 %multiply_reduce_fusion = (f32[2]{0:T(128)S(1)}, f32[2,512,512]{2,1,0:T(8,128)}) fusion(f32[2,512,512]{2,1,0:T(8,128)} %fusion.6, f32[2,512,512]{2,1,0:T(8,128)} %copy-done.10, f32[2,512,512]{2,1,0:T(8,128)} %copy-done.2, f32[2]{0:T(128)S(1)} %add_sqrt_fusion, f32[2,512,512]{2,1,0:T(8,128)} %multiply_add_fusion.1), kind=kOutput, calls=%fused_computation.7 | convolution fusion | flops 1084751872 | bytes 10485776 | tf_op jit(solution)/shard_map/vmap()/dot_general | solution.py:15
  138.5 0.4 multiply_reduce_fusion.1
  138.9 1.9 multiply_convert_fusion
  140.8 1.1 copy.20
  141.9 34.3 %all_to_all.34 = bf16[2,512,512]{2,0,1:T(2,128)(2,1)S(1)} all-to-all(bf16[2,512,512]{2,0,1:T(2,128)(2,1)S(1)} %copy.20), channel_id=1, replica_groups=mesh['dp'=4,'mp'=64] {'mp'}, dimensions={1} | all-to-all | bytes 2097152 | tf_op jit(solution)/shard_map/all_to_all | solution.py:91
  176.2 0.2 copy.41
  176.4 0.0 copy-start.3
  176.4 0.0 copy-start.4
  176.4 0.0 copy-start.5
  176.4 0.0 copy-start.7
  176.4 1.1 copy.22
  177.5 0.0 all-gather.2.cloned.1.call-update
  177.6 0.0 copy-done.3
  177.6 0.0 copy-done.4
  177.6 0.2 fusion.64
  177.8 0.1 fusion.40
  177.9 0.0 copy-done.5
  177.9 0.0 copy-done.7
  177.9 0.9 convolution_convert_fusion
  178.8 45.2 %all-gather.2.cloned.1.call-done = bf16[512,8,512]{2,1,0:T(8,128)(2,1)} async-done(((bf16[128,8,512]{2,1,0:T(8,128)(2,1)}), bf16[512,8,512]{2,1,0:T(8,128)(2,1)}) %all-gather.2.cloned.1.call-update) | async-done | bytes 4194320 | tf_op jit(solution)/shard_map/all_gather | solution.py:92
  224.0 4.4 %gather_fusion.1 = bf16[224,8,512]{2,1,0:T(8,128)(2,1)} fusion(bf16[512,8,512]{2,1,0:T(8,128)(2,1)} %all-gather.2.cloned.1.call-done, s32[1024]{0:T(1024)S(1)} %pad_clamp_fusion), kind=kCustom, calls=%fused_computation.1 | custom fusion | bytes 3670912 | tf_op jit(solution)/shard_map/jit(_take)/gather | solution.py:93
  228.4 3.0 %broadcast_select_fusion = bf16[224,8,512]{2,1,0:T(8,128)(2,1)} fusion(bf16[224,8,512]{2,1,0:T(8,128)(2,1)} %gather_fusion.1, pred[224]{0:T(512)(128)(4,1)S(1)} %compare_and_fusion), kind=kLoop, calls=%fused_computation.17 | loop fusion | flops 917504 | bytes 3670240 | tf_op jit(solution)/shard_map/jit(_take)/select_n | solution.py:93
  (13 shorter events, 0.1 us)
Async XLA Ops:
  7.2 2.2 copy-start
  7.2 62.2 %reduce-scatter.2.cloned.1.call-start = ((), (), s32[]{:S(2)}) async-start(), calls=%async_computation.3 | async-start | bytes 5242880 | tf_op jit(solution)/shard_map/reduce_scatter | solution.py:82
  18.1 205.8 %all-gather.2.cloned.1.call-start = ((), (), s32[]{:S(2)}) async-start(), calls=%async_computation.4 | async-start | bytes 5242880 | tf_op jit(solution)/shard_map/all_gather | solution.py:92
  69.4 39.5 %copy-start.6 = (f32[1,2,512,512]{3,2,1,0:T(8,128)S(1)}, f32[1,2,512,512]{3,2,1,0:T(8,128)}, u32[]{:S(2)}) copy-start(f32[1,2,512,512]{3,2,1,0:T(8,128)} %param.8) | copy-start | bytes 6291460
  109.9 1.3 copy-start.8
  111.2 1.4 copy-start.9
  112.6 2.1 copy-start.1
  115.8 1.3 copy-start.2
  117.2 1.3 copy-start.10
  176.4 1.2 copy-start.3
  176.4 1.2 copy-start.4
  176.4 1.5 copy-start.5
  176.4 1.5 copy-start.7
Sparse Core Ops, SparseCore 0:
  18.3 51.0 reduce-scatter.1
  177.7 46.2 all-gather.1

commit v2 on v1

--- a/solution.py
+++ b/solution.py
@@ -1,14 +1,18 @@
+import functools
 import math
 
 import jax
 import jax.numpy as jnp
 from jax import lax
+from jax.experimental import pallas as pl
+from jax.experimental.pallas import tpu as pltpu
 from jax.sharding import PartitionSpec as P
 
 HD = 128
-
-
 BETA = 0.9
+MESH = pl.DeviceIdType.MESH
+VMEM = pltpu.VMEM
+SMEM = pltpu.SMEM
 
 
 def narrow(left, right):
@@ -61,36 +65,354 @@
     return mixed.astype(jnp.bfloat16).reshape(query_vectors.shape)
 
 
+def to_slab(rows):
+    half = rows.shape[1] // 2
+    return jnp.concatenate([rows[:, :half], rows[:, half:]], axis=0)
+
+
+def from_slab(slab):
+    half = slab.shape[0] // 2
+    return jnp.concatenate([slab[:half], slab[half:]], axis=1)
+
+
+def loop(count, body, unroll=1):
+    def step(index, carry):
+        body(index)
+        return carry
+
+    lax.fori_loop(0, count, step, 0, unroll=unroll)
+
+
+class Ring:
+    def __init__(self, caps):
+        self.caps = caps
+        self.total = sum(caps)
+        here = lax.axis_index("dp")
+        self.right = {"dp": lax.rem(here + 1, 4)}
+        self.left = {"dp": lax.rem(here + 3, 4)}
+
+    def halves(self, chunk):
+        first = self.caps[chunk] // 2
+        return pl.ds(0, first), pl.ds(first, self.caps[chunk] - first)
+
+    def start(self, chunk):
+        return sum(self.caps[:chunk])
+
+
+def remote(src, dst, send_sem, recv_sem, device):
+    return pltpu.make_async_remote_copy(
+        src_ref=src, dst_ref=dst, send_sem=send_sem, recv_sem=recv_sem, device_id=device, device_id_type=MESH
+    )
+
+
+def peer_of(me, step, count):
+    if count != 64:
+        return lax.rem(me + step, count)
+    z, y, core = me // 8, (me // 2) % 4, me % 2
+    z = lax.rem(z + lax.rem(step, 8) * 3, 8)
+    y = lax.rem(y + lax.rem(step // 8, 4), 4)
+    core = lax.rem(core + step // 32, 2)
+    return z * 8 + y * 2 + core
+
+
+def greet(ring, count):
+    barrier = pltpu.get_barrier_semaphore()
+    me = lax.axis_index("mp")
+    for device in (ring.left, ring.right):
+        pl.semaphore_signal(barrier, inc=1, device_id=device, device_id_type=MESH)
+
+    def signal(step):
+        pl.semaphore_signal(
+            barrier, inc=1, device_id={"mp": peer_of(me, step + 1, count)}, device_id_type=MESH
+        )
+
+    loop(count - 1, signal)
+    pl.semaphore_wait(barrier, count + 1)
+
+
+def exchange_start(src, dst, send_sem, recv_sem, count):
+    me = lax.axis_index("mp")
+
+    def send(step):
+        peer = peer_of(me, step + 1, count)
+        remote(src.at[peer], dst.at[me], send_sem, recv_sem, {"mp": peer}).start()
+
+    loop(count - 1, send)
+    pltpu.make_async_copy(src.at[me], dst.at[me], recv_sem).start()
+
+
+def exchange_wait_recv(dst, recv_sem):
+    pltpu.make_async_copy(dst, dst, recv_sem).wait()
+
+
+def exchange_wait_send(src, send_sem, count):
+    part = src.at[pl.ds(0, count - 1)]
+    pltpu.make_async_copy(part, part, send_sem).wait()
+
+
+def scatter_copies(ring, chunk, buffers, send, recv):
+    first, second = ring.halves(chunk)
+    xs, tl, tr, fl, fr = buffers
+    plan = (
+        (xs.at[2, first], tl.at[first], ring.right),
+        (xs.at[2, second], tr.at[second], ring.left),
+        (xs.at[1, second], fl.at[second], ring.right),
+        (xs.at[3, first], fr.at[first], ring.left),
+        (xs.at[1, first], fl.at[first], ring.right),
+        (xs.at[3, second], fr.at[second], ring.left),
+    )
+    return [remote(s, t, send.at[chunk, k], recv.at[chunk, k], to) for k, (s, t, to) in enumerate(plan)]
+
+
+def gather_copies(ring, chunk, q, send, recv):
+    first, second = (
+        pl.ds(ring.start(chunk) + part.start, part.size) for part in ring.halves(chunk)
+    )
+    plan = (
+        (q.at[0, first], q.at[3, first], ring.right),
+        (q.at[0, second], q.at[1, second], ring.left),
+        (q.at[0, second], q.at[3, second], ring.right),
+        (q.at[0, first], q.at[1, first], ring.left),
+        (q.at[3, first], q.at[2, first], ring.right),
+        (q.at[1, second], q.at[2, second], ring.left),
+    )
+    return [remote(s, t, send.at[chunk, k], recv.at[chunk, k], to) for k, (s, t, to) in enumerate(plan)]
+
+
+def collect_kernel(
+    caps, count, src_ref, dense_ref, grads_ref, owned_ref,
+    *scratch,
+):
+    buffers = (scratch[:5], scratch[5:10])
+    out_slabs = scratch[10:12]
+    in_slabs = scratch[12:14]
+    x_send, x_recv, a_send, a_recv = scratch[14:]
+    ring = Ring(caps)
+    total = ring.total
+    here = lax.axis_index("dp")
+    greet(ring, count)
+
+    def pack(chunk, relative, part):
+        base = lax.rem(here + relative, 4) * total + ring.start(chunk) + part.start
+        xs = buffers[chunk][0]
+
+        def one(index):
+            block = src_ref[base + index]
+            xs[relative, part.start + index] = to_slab(grads_ref[block].astype(jnp.float32)).astype(jnp.bfloat16)
+
+        loop(part.size, one, unroll=4)
+
+    def add(chunk, relative, arrived, part):
+        xs = buffers[chunk][0]
+
+        def one(index):
+            at = part.start + index
+            both = xs[relative, at].astype(jnp.float32) + arrived[at].astype(jnp.float32)
+            xs[relative, at] = both.astype(jnp.bfloat16)
+
+        loop(part.size, one, unroll=4)
+
+    copies = [scatter_copies(ring, chunk, buffers[chunk], x_send, x_recv) for chunk in range(2)]
+
+    def open_chunk(chunk):
+        first, second = ring.halves(chunk)
+        for relative, part, copy in ((2, first, 0), (2, second, 1), (1, second, 2), (3, first, 3)):
+            pack(chunk, relative, part)
+            copies[chunk][copy].start()
+        pack(chunk, 1, first)
+        pack(chunk, 3, second)
+
+    def relay(chunk):
+        first, second = ring.halves(chunk)
+        copies[chunk][0].wait_recv()
+        add(chunk, 1, buffers[chunk][1], first)
+        copies[chunk][4].start()
+        copies[chunk][1].wait_recv()
+        add(chunk, 3, buffers[chunk][2], second)
+        copies[chunk][5].start()
+
+    def finish(chunk):
+        for copy in range(2, 6):
+            copies[chunk][copy].wait_recv()
+        xs, _, _, fl, fr = buffers[chunk]
+
+        def one(owner):
+            place = dense_ref[chunk * count + owner]
+            at = jnp.maximum(place, 0)
+            whole = xs[0, at].astype(jnp.float32) + fl[at].astype(jnp.float32) + fr[at].astype(jnp.float32)
+            out_slabs[chunk][owner] = jnp.where(place >= 0, whole, 0.0).astype(jnp.bfloat16)
+
+        loop(count, one, unroll=4)
+        exchange_start(out_slabs[chunk], in_slabs[chunk], a_send.at[chunk], a_recv.at[chunk], count)
+
+    open_chunk(0)
+    relay(0)
+    open_chunk(1)
+    for chunk in range(2):
+        for part in ring.halves(chunk):
+            pack(chunk, 0, part)
+    finish(0)
+    relay(1)
+    finish(1)
+
+    for chunk in range(2):
+        exchange_wait_recv(in_slabs[chunk], a_recv.at[chunk])
+
+        def place(pair):
+            upper = from_slab(in_slabs[chunk][2 * pair].astype(jnp.float32))
+            lower = from_slab(in_slabs[chunk][2 * pair + 1].astype(jnp.float32))
+            rows = pl.ds(pl.multiple_of(pair * 16, 16), 16)
+            owned_ref[chunk, rows] = jnp.concatenate([upper, lower], axis=0).astype(jnp.bfloat16)
+
+        loop(count // 2, place, unroll=2)
+    for chunk in range(2):
+        for copy in copies[chunk]:
+            copy.wait_send()
+        exchange_wait_send(out_slabs[chunk], a_send.at[chunk], count)
+
+
+def collect(grads, src, dense, caps, count):
+    total = sum(caps)
+    blocks, rows, columns = grads.shape
+    slab = (2 * rows, columns // 2)
+    return pl.pallas_call(
+        functools.partial(collect_kernel, caps, count),
+        out_shape=jax.ShapeDtypeStruct((2, count * rows, columns), jnp.bfloat16),
+        in_specs=[pl.BlockSpec(memory_space=SMEM)] * 2 + [pl.BlockSpec(memory_space=VMEM)],
+        out_specs=pl.BlockSpec(memory_space=VMEM),
+        scratch_shapes=[
+            *[
+                VMEM(lead + slab, jnp.bfloat16)
+                for cap in caps
+                for lead in ((4, cap), (cap,), (cap,), (cap,), (cap,))
+            ],
+            *[VMEM((count,) + slab, jnp.bfloat16)] * 4,
+            pltpu.SemaphoreType.DMA((2, 6)),
+            pltpu.SemaphoreType.DMA((2, 6)),
+            pltpu.SemaphoreType.DMA((2,)),
+            pltpu.SemaphoreType.DMA((2,)),
+        ],
+        compiler_params=pltpu.CompilerParams(
+            collective_id=0, has_side_effects=True, vmem_limit_bytes=48 * 2**20
+        ),
+    )(src, dense, grads)
+
+
+def spread_kernel(
+    caps, count, packed_ref, place_ref, ready_ref, update_ref,
+    *scratch,
+):
+    out_slabs, in_slabs = scratch[0:2], scratch[2:4]
+    q, x_send, x_recv, a_send, a_recv = scratch[4:]
+    ring = Ring(caps)
+    greet(ring, count)
+    for chunk in range(2):
+
+        def cut(pair):
+            rows = pl.ds(pl.multiple_of(pair * 16, 16), 16)
+            both = ready_ref[chunk, rows].astype(jnp.float32)
+            out_slabs[chunk][2 * pair] = to_slab(both[:8]).astype(jnp.bfloat16)
+            out_slabs[chunk][2 * pair + 1] = to_slab(both[8:]).astype(jnp.bfloat16)
+
+        loop(count // 2, cut, unroll=2)
+        exchange_start(out_slabs[chunk], in_slabs[chunk], a_send.at[chunk], a_recv.at[chunk], count)
+
+    copies = [gather_copies(ring, chunk, q, x_send, x_recv) for chunk in range(2)]
+
+    def open_chunk(chunk):
+        exchange_wait_recv(in_slabs[chunk], a_recv.at[chunk])
+        first, second = ring.halves(chunk)
+        for part, starts in ((first, (0, 3)), (second, (1, 2))):
+
+            def one(index):
+                at = ring.start(chunk) + part.start + index
+                q[0, at] = in_slabs[chunk][packed_ref[at]]
+
+            loop(part.size, one, unroll=4)
+            for copy in starts:
+                copies[chunk][copy].start()
+
+    def forward(chunk):
+        for arrived, onward in ((0, 4), (1, 5)):
+            copies[chunk][arrived].wait_recv()
+            copies[chunk][onward].start()
+
+    open_chunk(0)
+    forward(0)
+    open_chunk(1)
+    forward(1)
+    for chunk in range(2):
+        for copy in range(2, 6):
+            copies[chunk][copy].wait_recv()
+
+    def settle(block):
+        place = place_ref[block]
+        slab = q[place // ring.total, place % ring.total]
+        update_ref[block] = from_slab(slab.astype(jnp.float32)).astype(jnp.bfloat16)
+
+    loop(update_ref.shape[0], settle, unroll=4)
+    for chunk in range(2):
+        for copy in copies[chunk]:
+            copy.wait_send()
+        exchange_wait_send(out_slabs[chunk], a_send.at[chunk], count)
+
+
+def spread(ready, packed, place, caps, count, rows):
+    total = sum(caps)
+    columns = ready.shape[2]
+    slab = (2 * rows, columns // 2)
+    return pl.pallas_call(
+        functools.partial(spread_kernel, caps, count),
+        out_shape=jax.ShapeDtypeStruct((place.shape[0], rows, columns), jnp.bfloat16),
+        in_specs=[pl.BlockSpec(memory_space=SMEM)] * 2 + [pl.BlockSpec(memory_space=VMEM)],
+        out_specs=pl.BlockSpec(memory_space=VMEM),
+        scratch_shapes=[
+            *[VMEM((count,) + slab, jnp.bfloat16)] * 4,
+            VMEM((4, total) + slab, jnp.bfloat16),
+            pltpu.SemaphoreType.DMA((2, 6)),
+            pltpu.SemaphoreType.DMA((2, 6)),
+            pltpu.SemaphoreType.DMA((2,)),
+            pltpu.SemaphoreType.DMA((2,)),
+        ],
+        compiler_params=pltpu.CompilerParams(
+            collective_id=1, has_side_effects=True, vmem_limit_bytes=48 * 2**20
+        ),
+    )(packed, place, ready)
+
+
+def tables(assign, count):
+    here = lax.axis_index("dp")
+    total = 2 * count
+    slots = 4 * total
+    source = (
+        jnp.full((slots,), -1, jnp.int32)
+        .at[assign]
+        .set(jnp.arange(assign.shape[0], dtype=jnp.int32))
+    )
+    ordered = source.reshape(4, count, 2).transpose(0, 2, 1).reshape(4, total)
+    src = jnp.maximum(ordered, 0).reshape(slots)
+    mine = lax.dynamic_index_in_dim(ordered, here, 0, keepdims=False)
+    numbers = jnp.arange(total, dtype=jnp.int32)
+    dense = jnp.where(mine >= 0, numbers % count, -1)
+    packed = numbers % count
+    replica, inside = assign // total, assign % total
+    relative = (replica - here + 4) % 4
+    place = relative * total + (inside % 2) * count + inside // 2
+    return src, dense, packed, place
+
+
 def body(partial_grads, stat_left, stat_right, assign, query_vectors, key_vectors, value_vectors):
-    replica_count = lax.axis_size("dp")
-    column_count = lax.axis_size("mp")
-    capacity = stat_left.shape[1]
-    block_order = partial_grads.shape[3]
-    sliver_rows = partial_grads.shape[2]
-    total_slots = replica_count * column_count * capacity
-    block_count = assign.shape[0]
-    source = (
-        jnp.full((total_slots,), -1, jnp.int32)
-        .at[assign]
-        .set(jnp.arange(block_count, dtype=jnp.int32))
-    )
-    picked = jnp.take(partial_grads[0], jnp.maximum(source, 0), axis=0)
-    packed = jnp.where((source >= 0)[:, None, None], picked, jnp.zeros((), jnp.bfloat16))
-    grouped = packed.astype(jnp.float32).reshape(
-        replica_count, column_count * capacity, sliver_rows, block_order
-    )
-    summed = lax.psum_scatter(grouped.astype(jnp.bfloat16), "dp", scatter_dimension=0, tiled=True)
-    rounded = summed.reshape(column_count, capacity, sliver_rows, block_order)
-    owned = lax.all_to_all(rounded, "mp", split_axis=0, concat_axis=2, tiled=True)[0]
+    count = lax.axis_size("mp")
+    caps = (count, count)
+    src, dense, packed, place = tables(assign, count)
+    owned = collect(partial_grads[0], src, dense, caps, count)
     left_gram = jnp.einsum("sik,sjk->sij", owned, owned, preferred_element_type=jnp.float32)
     right_gram = jnp.einsum("ski,skj->sij", owned, owned, preferred_element_type=jnp.float32)
     left_next = BETA * stat_left[0] + (1.0 - BETA) * left_gram
     right_next = BETA * stat_right[0] + (1.0 - BETA) * right_gram
     attended = local_attention(query_vectors, key_vectors, value_vectors)
     updates = jax.vmap(precondition)(owned, left_next, right_next)
-    returned = lax.all_to_all(updates, "mp", split_axis=1, concat_axis=0, tiled=True)
-    everywhere = lax.all_gather(returned, "dp", axis=0, tiled=True)
-    update = jnp.take(everywhere, assign, axis=0)
+    update = spread(updates, packed, place, caps, count, partial_grads.shape[2])
     return (left_next[None], right_next[None], update, attended)
 
 

time: 240 us -> 165 us (0.69)
  Pallas kernels: 0 us -> 128 us
  waiting for transfers between devices: 96.4 us -> 0 us
  blocking collectives: 73.7 us -> 0 us
  between operations: 14.2 us -> 0.78 us
  other arithmetic: 11.5 us -> 1.59 us
  local copies, waits for them, and re-layouts: 15.3 us -> 8.1 us
    pallas_call x0 -> x2, Pallas kernels: none -> 128 us  [the longest x1 64.8 us: spread(): pl.pallas_call(functools.partial(spread_kernel, caps, count), out_shape=j...]
    all_to_all x2 -> x0, blocking collectives: 73.7 us -> none  [the longest x1 39.5 us: body(): lax.all_to_all(rounded, 'mp', split_axis=0, concat_axis=2, tiled=True)[0]]
    reduce_scatter x1 -> x0, waiting for transfers between devices: 51.2 us -> none  [body(): lax.psum_scatter(grouped.astype(jnp.bfloat16), 'dp', scatter_dimension=0,...]
    all_gather x1 -> x0, waiting for transfers between devices: 45.2 us -> none  [body(): everywhere = lax.all_gather(returned, 'dp', axis=0, tiled=True)]
    select_n x3 -> x2, other arithmetic: 9.1 us -> 0.01 us  [tables(): dense = jnp.where(mine >= 0, numbers % count, -1)]
    gather x2 -> x0, local copies, waits for them, and re-layouts: 7.87 us -> none  [the longest x1 4.39 us: body(): update = jnp.take(everywhere, assign, axis=0)]
    unnamed x22 -> x21, local copies, waits for them, and re-layouts: 3.74 us -> 6.39 us
  transfers between devices with their start and end apart: 2 -> 0, of which waited for: 2 -> 0; matrix products, arithmetic and copies ran while one was open for 0% -> 0% of each run, Pallas kernels for 0% -> 0%
where the time goes in v2:
time: 165 us
  Pallas kernels  128 us (78%)
  matrix products  26.1 us (16%)
  local copies, waits for them, and re-layouts  8.1 us (5%)
    pallas_call x1, Pallas kernels, spread(): pl.pallas_call(functools.partial(spread_kernel, caps, count), out_shape=j...  64.8 us
    pallas_call x1, Pallas kernels, collect(): pl.pallas_call(functools.partial(collect_kernel, caps, count), out_shape=...  63.2 us
    dot_general x6, matrix products, narrow(): jnp.matmul(left.astype(jnp.bfloat16), right.astype(jnp.bfloat16), preferr...  22.9 us
    unnamed x21, local copies, waits for them, and re-layouts  6.39 us

profile of v2, /device:TPU:2, one launch (start us, length us, event | category | flops | bytes accessed | tf_op | source)
XLA Modules:
  0.0 164.6 jit_solution(17143887580136356571)
XLA Ops:
  0.6 0.0 copy-start
  0.7 0.7 fusion.39
  1.4 1.3 scatter_custom_fusion
  2.7 0.1 reshape.77
  2.8 0.1 copy.16
  2.9 0.1 reshape.78
  3.1 0.1 max.12.src_ref
  3.1 0.0 copy-start.1
  3.1 1.5 copy-done.1
  4.6 0.0 copy-start.2
  4.6 63.2 %shard_map.102 = bf16[2,512,512]{2,1,0:T(8,128)(2,1)S(1)} custom-call(s32[512]{0:T(512)S(1)} %max.12.src_ref, s32[128]{0:T(128)S(1)} %bitcast_select_fusion.dense_ref, bf16[224,8,512]{2,1,0:T(8,128)(2,1)S(1)} %bitcast.19), custom_call_target="tpu_custom_call" | custom-call | tf_op jit(solution)/shard_map/pallas_call | solution.py:278
  67.9 0.0 copy-done.2
  67.9 1.0 multiply_reduce_fusion.2
  68.9 0.0 copy-start.4
  68.9 0.8 fusion.34
  69.7 0.5 copy-done.4
  70.2 0.0 copy-start.9
  70.2 1.3 copy-done.9
  71.5 2.1 %fusion.24 = f32[2,512,512]{2,1,0:T(8,128)} fusion(f32[2,512,512]{2,1,0:T(8,128)S(1)} %fusion.34, f32[2,512,512]{2,1,0:T(8,128)S(1)} %get-tuple-element.7, f32[2]{0:T(128)S(1)} %add_sqrt_fusion.1), kind=kOutput, calls=%fused_computation.33 | convolution fusion | flops 538443776 | bytes 6291464 | tf_op jit(solution)/shard_map/vmap()/dot_general | solution.py:19
  73.6 0.0 copy-start.3
  73.6 8.5 %fusion = f32[2,512,512]{2,1,0:T(8,128)} fusion(bf16[2,512,512]{2,1,0:T(8,128)(2,1)S(1)} %shard_map.102, f32[2,512,512]{2,1,0:T(8,128)} %fusion.24, f32[2,512,512]{2,1,0:T(8,128)} %copy-done.9, f32[2,512,512]{2,1,0:T(8,128)} %copy-done.4, f32[2]{0:T(128)S(1)} %add_sqrt_fusion.1), kind=kOutput, calls=%fused_computation.3 | convolution fusion | flops 1083703296 | bytes 9437192 | tf_op jit(solution)/shard_map/vmap()/dot_general | solution.py:19
  82.1 0.0 copy-done.3
  82.1 1.1 multiply_reduce_fusion.1
  83.2 0.0 copy-start.5
  83.2 0.8 fusion.31
  84.0 0.5 copy-done.5
  84.5 0.0 copy-start.8
  84.5 1.3 copy-done.8
  85.9 2.1 %fusion.5 = f32[2,512,512]{2,1,0:T(8,128)} fusion(f32[2,512,512]{2,1,0:T(8,128)S(1)} %fusion.31, f32[2,512,512]{2,1,0:T(8,128)S(1)} %get-tuple-element.9, f32[2]{0:T(128)S(1)} %add_sqrt_fusion), kind=kOutput, calls=%fused_computation.20 | convolution fusion | flops 538443776 | bytes 6291464 | tf_op jit(solution)/shard_map/vmap()/dot_general | solution.py:19
  88.0 8.6 %multiply_reduce_fusion = (f32[2]{0:T(128)S(1)}, f32[2,512,512]{2,1,0:T(8,128)S(1)}) fusion(f32[2,512,512]{2,1,0:T(8,128)} %fusion.5, f32[2,512,512]{2,1,0:T(8,128)} %copy-done.8, f32[2,512,512]{2,1,0:T(8,128)} %copy-done.5, f32[2]{0:T(128)S(1)} %add_sqrt_fusion, f32[2,512,512]{2,1,0:T(8,128)} %fusion), kind=kOutput, calls=%fused_computation.8 | convolution fusion | flops 1084751872 | bytes 10485776 | tf_op jit(solution)/shard_map/vmap()/dot_general | solution.py:19
  96.6 0.4 fusion.1
  97.0 0.3 multiply_convert_fusion.ready_ref
  97.3 0.0 copy-start.6
  97.3 0.0 copy-start.7
  97.3 64.8 %shard_map.103 = bf16[224,8,512]{2,1,0:T(8,128)(2,1)S(1)} custom-call(s32[128]{0:T(128)S(1)} %and_select_fusion.5.packed_ref, s32[224]{0:T(256)S(1)} %get-tuple-element.4.place_ref, bf16[2,512,512]{2,1,0:T(8,128)(2,1)S(1)} %multiply_convert_fusion.ready_ref), custom_call_target="tpu_custom_call" | custom-call | tf_op jit(solution)/shard_map/pallas_call | solution.py:364
  162.1 0.0 copy-done
  162.1 0.0 copy-done.6
  162.1 0.2 fusion.65
  162.4 0.1 fusion.36
  162.4 0.0 copy-done.7
  162.4 0.9 convolution_convert_fusion
  163.3 1.2 copy.22
  (9 shorter events, 0.1 us)
Async XLA Ops:
  0.6 161.5 %copy-start = (bf16[256,128]{1,0:T(8,128)(2,1)S(1)}, bf16[256,128]{1,0:T(8,128)(2,1)}, u32[]{:S(2)}) copy-start(bf16[256,128]{1,0:T(8,128)(2,1)} %param.11) | copy-start | bytes 196612
  3.1 1.5 copy-start.1
  4.6 63.2 %copy-start.2 = (f32[1,2,512,512]{3,2,1,0:T(8,128)S(1)}, f32[1,2,512,512]{3,2,1,0:T(8,128)}, u32[]{:S(2)}) copy-start(f32[1,2,512,512]{3,2,1,0:T(8,128)} %param.8) | copy-start | bytes 6291460
  68.9 1.3 copy-start.4
  70.2 1.3 copy-start.9
  73.6 8.5 %copy-start.3 = (f32[1,2,512,512]{3,2,1,0:T(8,128)S(1)}, f32[1,2,512,512]{3,2,1,0:T(8,128)}, u32[]{:S(2)}) copy-start(f32[1,2,512,512]{3,2,1,0:T(8,128)} %param.9) | copy-start | bytes 6291460
  83.2 1.3 copy-start.5
  84.5 1.3 copy-start.8
  97.3 64.8 %copy-start.6 = (bf16[256,128]{1,0:T(8,128)(2,1)S(1)}, bf16[256,128]{1,0:T(8,128)(2,1)}, u32[]{:S(2)}) copy-start(bf16[256,128]{1,0:T(8,128)(2,1)} %param.12) | copy-start | bytes 196612
  97.3 65.1 %copy-start.7 = (bf16[256,128]{1,0:T(8,128)(2,1)S(1)}, bf16[256,128]{1,0:T(8,128)(2,1)}, u32[]{:S(2)}) copy-start(bf16[256,128]{1,0:T(8,128)(2,1)} %param.13) | copy-start | bytes 196612

commit v3 on v2

v3 whole, which is shorter than its diff:
```python
import functools
import math

import jax
import jax.numpy as jnp
from jax import lax
from jax.experimental import pallas as pl
from jax.experimental.pallas import tpu as pltpu
from jax.sharding import PartitionSpec as P

BETA = 0.9
MESH = pl.DeviceIdType.MESH
VMEM = pltpu.VMEM
SMEM = pltpu.SMEM


def to_slab(rows):
    half = rows.shape[1] // 2
    return jnp.concatenate([rows[:, :half], rows[:, half:]], axis=0)


def from_slab(slab):
    half = slab.shape[0] // 2
    return jnp.concatenate([slab[:half], slab[half:]], axis=1)


def loop(count, body, unroll=1):
    def step(index, carry):
        body(index)
        return carry

    lax.fori_loop(0, count, step, 0, unroll=unroll)


class Ring:
    def __init__(self, caps):
        self.caps = caps
        self.total = sum(caps)
        here = lax.axis_index("dp")
        self.right = {"dp": lax.rem(here + 1, 4)}
        self.left = {"dp": lax.rem(here + 3, 4)}

    def halves(self, chunk):
        first = self.caps[chunk] // 2
        return pl.ds(0, first), pl.ds(first, self.caps[chunk] - first)

    def start(self, chunk):
        return sum(self.caps[:chunk])


def remote(src, dst, send_sem, recv_sem, device):
    return pltpu.make_async_remote_copy(
        src_ref=src, dst_ref=dst, send_sem=send_sem, recv_sem=recv_sem, device_id=device, device_id_type=MESH
    )


def peer_of(me, step, count):
    if count != 64:
        return lax.rem(me + step, count)
    z, y, core = me // 8, (me // 2) % 4, me % 2
    z = lax.rem(z + lax.rem(step, 8) * 3, 8)
    y = lax.rem(y + lax.rem(step // 8, 4), 4)
    core = lax.rem(core + step // 32, 2)
    return z * 8 + y * 2 + core


def greet(ring, count):
    barrier = pltpu.get_barrier_semaphore()
    me = lax.axis_index("mp")
    for device in (ring.left, ring.right):
        pl.semaphore_signal(barrier, inc=1, device_id=device, device_id_type=MESH)

    def signal(step):
        pl.semaphore_signal(
            barrier, inc=1, device_id={"mp": peer_of(me, step + 1, count)}, device_id_type=MESH
        )

    loop(count - 1, signal)
    pl.semaphore_wait(barrier, count + 1)


def exchange_start(src, dst, send_sem, recv_sem, count):
    me = lax.axis_index("mp")

    def send(step):
        peer = peer_of(me, step + 1, count)
        remote(src.at[peer], dst.at[me], send_sem, recv_sem, {"mp": peer}).start()

    loop(count - 1, send)
    pltpu.make_async_copy(src.at[me], dst.at[me], recv_sem).start()


def exchange_wait_recv(dst, recv_sem):
    pltpu.make_async_copy(dst, dst, recv_sem).wait()


def exchange_wait_send(src, send_sem, count):
    part = src.at[pl.ds(0, count - 1)]
    pltpu.make_async_copy(part, part, send_sem).wait()


def scatter_copies(ring, chunk, buffers, send, recv):
    first, second = ring.halves(chunk)
    xs, tl, tr, fl, fr = buffers
    plan = (
        (xs.at[2, first], tl.at[first], ring.right),
        (xs.at[2, second], tr.at[second], ring.left),
        (xs.at[1, second], fl.at[second], ring.right),
        (xs.at[3, first], fr.at[first], ring.left),
        (xs.at[1, first], fl.at[first], ring.right),
        (xs.at[3, second], fr.at[second], ring.left),
    )
    return [remote(s, t, send.at[chunk, k], recv.at[chunk, k], to) for k, (s, t, to) in enumerate(plan)]


def gather_copies(ring, chunk, q, send, recv):
    first, second = (
        pl.ds(ring.start(chunk) + part.start, part.size) for part in ring.halves(chunk)
    )
    plan = (
        (q.at[0, first], q.at[3, first], ring.right),
        (q.at[0, second], q.at[1, second], ring.left),
        (q.at[0, second], q.at[3, second], ring.right),
        (q.at[0, first], q.at[1, first], ring.left),
        (q.at[3, first], q.at[2, first], ring.right),
        (q.at[1, second], q.at[2, second], ring.left),
    )
    return [remote(s, t, send.at[chunk, k], recv.at[chunk, k], to) for k, (s, t, to) in enumerate(plan)]


LINEAR = -(5.0 / 16.0 + 3125.0 / 4096.0)
SQUARE = 3125.0 / 4096.0
CUBE = -1250.0 / 4096.0


def dot(left, right, dims=((1,), (0,))):
    return lax.dot_general(left, right, (dims, ((), ())), preferred_element_type=jnp.float32)


def column_parts(order, body):
    width = 256

    def one(part):
        body(pl.ds(pl.multiple_of(part * width, width), width))

    loop(order // width, one)


def excess(gram, stat, result, first_b, second, second_b, third_b, tail_b, out):
    order = stat.shape[0]

    def blend(columns):
        result[:, columns] = BETA * stat[:, columns] + (1.0 - BETA) * gram(columns)

    column_parts(order, blend)
    whole = result[...]
    scale = 1.0 / jnp.sqrt(jnp.sum(whole * whole) + 1e-06)
    first_b[...] = (result[...] * scale).astype(jnp.bfloat16)

    def square(columns):
        value = dot(first_b[...], first_b[:, columns])
        second[:, columns] = value
        second_b[:, columns] = value.astype(jnp.bfloat16)

    column_parts(order, square)

    def cube(columns):
        third = dot(second_b[...], first_b[:, columns])
        first = result[:, columns] * scale
        two = second[:, columns]
        third_b[:, columns] = third.astype(jnp.bfloat16)
        tail_b[:, columns] = ((250.0 * first - 25.0 * two + third) * (1.0 / 4096.0)).astype(jnp.bfloat16)
        second[:, columns] = LINEAR * first + SQUARE * two + CUBE * third

    column_parts(order, cube)

    def last(columns):
        out[:, columns] = (second[:, columns] + dot(tail_b[...], third_b[:, columns])).astype(jnp.bfloat16)

    column_parts(order, last)


def attend(query, key, value, out):
    length, width = query.shape
    scores = dot(query[...], key[...], ((1,), (1,))) * (1.0 / math.sqrt(width))
    causal = lax.broadcasted_iota(jnp.int32, (length, length), 0) >= lax.broadcasted_iota(
        jnp.int32, (length, length), 1
    )
    scores = jnp.where(causal, scores, -jnp.inf)
    weights = jnp.exp(scores - jnp.max(scores, axis=-1, keepdims=True))
    probs = (weights / jnp.sum(weights, axis=-1, keepdims=True)).astype(jnp.bfloat16)
    out[...] = dot(probs, value[...]).astype(jnp.bfloat16)


def step_kernel(
    caps, count, src_ref, dense_ref, packed_ref, place_ref,
    grads_ref, stat_left, stat_right, query, key, value,
    left_next, right_next, update_ref, attended,
    *scratch,
):
    buffers = (scratch[:5], scratch[5:10])
    out_slabs, in_slabs, out_back, in_back = scratch[10:12], scratch[12:14], scratch[14:16], scratch[16:18]
    q, block, first_b, second, second_b, third_b, tail_b, left_b, right_b, half_b = scratch[18:28]
    x_send, x_recv, a_send, a_recv, g_send, g_recv, b_send, b_recv = scratch[28:]
    ring = Ring(caps)
    total = ring.total
    here = lax.axis_index("dp")
    greet(ring, count)

    def pack(chunk, relative, part):
        base = lax.rem(here + relative, 4) * total + ring.start(chunk) + part.start
        xs = buffers[chunk][0]

        def one(index):
            number = src_ref[base + index]
            xs[relative, part.start + index] = to_slab(grads_ref[number].astype(jnp.float32)).astype(jnp.bfloat16)

        loop(part.size, one, unroll=4)

    def add(chunk, relative, arrived, part):
        xs = buffers[chunk][0]

        def one(index):
            at = part.start + index
            both = xs[relative, at].astype(jnp.float32) + arrived[at].astype(jnp.float32)
            xs[relative, at] = both.astype(jnp.bfloat16)

        loop(part.size, one, unroll=4)

    reduce = [scatter_copies(ring, chunk, buffers[chunk], x_send, x_recv) for chunk in range(2)]
    gather = [gather_copies(ring, chunk, q, g_send, g_recv) for chunk in range(2)]

    def open_chunk(chunk):
        first, second_half = ring.halves(chunk)
        for relative, part, copy in ((2, first, 0), (2, second_half, 1), (1, second_half, 2), (3, first, 3)):
            pack(chunk, relative, part)
            reduce[chunk][copy].start()
        pack(chunk, 1, first)
        pack(chunk, 3, second_half)

    def relay(chunk):
        first, second_half = ring.halves(chunk)
        reduce[chunk][0].wait_recv()
        add(chunk, 1, buffers[chunk][1], first)
        reduce[chunk][4].start()
        reduce[chunk][1].wait_recv()
        add(chunk, 3, buffers[chunk][2], second_half)
        reduce[chunk][5].start()

    def finish(chunk):
        for copy in range(2, 6):
            reduce[chunk][copy].wait_recv()
        xs, _, _, fl, fr = buffers[chunk]

        def one(owner):
            place = dense_ref[chunk * count + owner]
            at = jnp.maximum(place, 0)
            whole = xs[0, at].astype(jnp.float32) + fl[at].astype(jnp.float32) + fr[at].astype(jnp.float32)
            out_slabs[chunk][owner] = jnp.where(place >= 0, whole, 0.0).astype(jnp.bfloat16)

        loop(count, one, unroll=4)
        exchange_start(out_slabs[chunk], in_slabs[chunk], a_send.at[chunk], a_recv.at[chunk], count)

    def precondition(chunk):
        exchange_wait_recv(in_slabs[chunk], a_recv.at[chunk])

        def place(pair):
            upper = from_slab(in_slabs[chunk][2 * pair].astype(jnp.float32))
            lower = from_slab(in_slabs[chunk][2 * pair + 1].astype(jnp.float32))
            rows = pl.ds(pl.multiple_of(pair * 16, 16), 16)
            block[rows] = jnp.concatenate([upper, lower], axis=0).astype(jnp.bfloat16)

        loop(count // 2, place, unroll=2)
        order = block.shape[0]
        spare = (first_b, second, second_b, third_b, tail_b)
        excess(
            lambda columns: dot(block[...], block[columns], ((1,), (1,))),
            stat_left.at[chunk], left_next.at[chunk], *spare, left_b,
        )
        excess(
            lambda columns: dot(block[...], block[:, columns], ((0,), (0,))),
            stat_right.at[chunk], right_next.at[chunk], *spare, right_b,
        )

        def left_side(columns):
            part = (25.0 / 16.0) * block[:, columns].astype(jnp.float32) + dot(left_b[...], block[:, columns])
            second[:, columns] = part
            half_b[:, columns] = part.astype(jnp.bfloat16)

        column_parts(order, left_side)

        def right_side(columns):
            second[:, columns] = (25.0 / 16.0) * second[:, columns] + dot(half_b[...], right_b[:, columns])

        column_parts(order, right_side)
        raw = second[...]
        widened = block[...].astype(jnp.float32)
        mean_raw = jnp.sum(raw * raw) * (1.0 / raw.size)
        mean_block = jnp.sum(widened * widened) * (1.0 / raw.size)
        scale = jnp.sqrt((mean_block + 1e-06) / (mean_raw + 1e-06))

        def cut(owner):
            rows = pl.ds(pl.multiple_of(owner * 8, 8), 8)
            out_back[chunk][owner] = to_slab(second[rows] * scale).astype(jnp.bfloat16)

        loop(count, cut, unroll=4)
        exchange_start(out_back[chunk], in_back[chunk], b_send.at[chunk], b_recv.at[chunk], count)

    def open_gather(chunk):
        exchange_wait_recv(in_back[chunk], b_recv.at[chunk])
        for part, starts in zip(ring.halves(chunk), ((0, 3), (1, 2))):

            def one(index):
                at = ring.start(chunk) + part.start + index
                q[0, at] = in_back[chunk][packed_ref[at]]

            loop(part.size, one, unroll=4)
            for copy in starts:
                gather[chunk][copy].start()

    def forward(chunk):
        for arrived, onward in ((0, 4), (1, 5)):
            gather[chunk][arrived].wait_recv()
            gather[chunk][onward].start()

    open_chunk(0)
    attend(query, key, value, attended)
    relay(0)
    open_chunk(1)
    for chunk in range(2):
        for part in ring.halves(chunk):
            pack(chunk, 0, part)
    finish(0)
    relay(1)
    finish(1)
    precondition(0)
    precondition(1)
    open_gather(0)
    forward(0)
    open_gather(1)
    forward(1)
    for chunk in range(2):
        for copy in range(2, 6):
            gather[chunk][copy].wait_recv()

    def settle(number):
        place = place_ref[number]
        slab = q[place // total, place % total]
        update_ref[number] = from_slab(slab.astype(jnp.float32)).astype(jnp.bfloat16)

    loop(update_ref.shape[0], settle, unroll=4)
    for chunk in range(2):
        for copy in reduce[chunk] + gather[chunk]:
            copy.wait_send()
        exchange_wait_send(out_slabs[chunk], a_send.at[chunk], count)
        exchange_wait_send(out_back[chunk], b_send.at[chunk], count)


def step(grads, stat_left, stat_right, query, key, value, src, dense, packed, place, caps, count):
    total = sum(caps)
    blocks, rows, columns = grads.shape
    order = stat_left.shape[1]
    slab = (2 * rows, columns // 2)
    narrow = VMEM((order, order), jnp.bfloat16)
    wide = VMEM((order, order), jnp.float32)
    dma = pltpu.SemaphoreType.DMA
    return pl.pallas_call(
        functools.partial(step_kernel, caps, count),
        out_shape=(
            jax.ShapeDtypeStruct(stat_left.shape, jnp.float32),
            jax.ShapeDtypeStruct(stat_right.shape, jnp.float32),
            jax.ShapeDtypeStruct(grads.shape, jnp.bfloat16),
            jax.ShapeDtypeStruct(query.shape, jnp.bfloat16),
        ),
        in_specs=[pl.BlockSpec(memory_space=SMEM)] * 4 + [pl.BlockSpec(memory_space=VMEM)] * 6,
        out_specs=[pl.BlockSpec(memory_space=VMEM)] * 4,
        scratch_shapes=[
            *[
                VMEM(lead + slab, jnp.bfloat16)
                for cap in caps
                for lead in ((4, cap), (cap,), (cap,), (cap,), (cap,))
            ],
            *[VMEM((count,) + slab, jnp.bfloat16)] * 8,
            VMEM((4, total) + slab, jnp.bfloat16),
            narrow, narrow, wide, narrow, narrow, narrow, narrow, narrow, narrow,
            dma((2, 6)), dma((2, 6)), dma((2,)), dma((2,)),
            dma((2, 6)), dma((2, 6)), dma((2,)), dma((2,)),
        ],
        compiler_params=pltpu.CompilerParams(
            collective_id=0, has_side_effects=True, vmem_limit_bytes=56 * 2**20
        ),
    )(src, dense, packed, place, grads, stat_left, stat_right, query, key, value)


def tables(assign, count):
    here = lax.axis_index("dp")
    total = 2 * count
    slots = 4 * total
    source = (
        jnp.full((slots,), -1, jnp.int32)
        .at[assign]
        .set(jnp.arange(assign.shape[0], dtype=jnp.int32))
    )
    ordered = source.reshape(4, count, 2).transpose(0, 2, 1).reshape(4, total)
    src = jnp.maximum(ordered, 0).reshape(slots)
    mine = lax.dynamic_index_in_dim(ordered, here, 0, keepdims=False)
    numbers = jnp.arange(total, dtype=jnp.int32)
    dense = jnp.where(mine >= 0, numbers % count, -1)
    packed = numbers % count
    replica, inside = assign // total, assign % total
    relative = (replica - here + 4) % 4
    place = relative * total + (inside % 2) * count + inside // 2
    return src, dense, packed, place


def body(partial_grads, stat_left, stat_right, assign, query_vectors, key_vectors, value_vectors):
    count = lax.axis_size("mp")
    caps = (count, count)
    src, dense, packed, place = tables(assign, count)
    left_next, right_next, update, attended = step(
        partial_grads[0], stat_left[0], stat_right[0], query_vectors, key_vectors, value_vectors,
        src, dense, packed, place, caps, count,
    )
    return (left_next[None], right_next[None], update, attended)


def solution(mesh):
    placed = (
        P("dp", None, "mp", None),
        P("dp", "mp", None, None),
        P("dp", "mp", None, None),
        P(),
        P("dp", "mp"),
        P("dp", "mp"),
        P("dp", "mp"),
    )
    return jax.shard_map(
        body,
        mesh=mesh,
        in_specs=placed,
        out_specs=(
            P("dp", "mp", None, None),
            P("dp", "mp", None, None),
            P(None, "mp", None),
            P("dp", "mp"),
        ),
        check_vma=False,
    )
```

time: 165 us -> 134 us (0.81)
  matrix products: 26.1 us -> 0 us
  Pallas kernels: 128 us -> 122 us
    dot_general x10 -> x0, matrix products: 26.1 us -> none  [the longest x6 22.9 us: narrow(): jnp.matmul(left.astype(jnp.bfloat16), right.astype(jnp.bfloat16), preferr...]
    pallas_call x2 -> x1, Pallas kernels: 128 us -> 122 us  [step(): pl.pallas_call(functools.partial(step_kernel, caps, count), out_shape=(ja...]
    unnamed x21 -> x10, local copies, waits for them, and re-layouts: 6.39 us -> 7.35 us
where the time goes in v3:
time: 134 us
  Pallas kernels  122 us (91%)
  local copies, waits for them, and re-layouts  9.63 us (7%)
  other arithmetic  1.8 us (1%)
    pallas_call x1, Pallas kernels, step(): pl.pallas_call(functools.partial(step_kernel, caps, count), out_shape=(ja...  122 us
    unnamed x10, local copies, waits for them, and re-layouts  7.35 us

profile of v3, /device:TPU:2, one launch (start us, length us, event | category | flops | bytes accessed | tf_op | source)
XLA Modules:
  0.0 134.3 jit_solution(1135295746451795084)
XLA Ops:
  0.6 1.3 fusion.2
  1.9 1.3 scatter_custom_fusion
  3.2 0.1 reshape.20
  3.4 0.1 copy.13
  3.5 0.1 reshape.21
  3.5 0.5 bitcast_select_fusion
  4.1 0.7 max.12.src_ref
  4.7 122.1 %shard_map.102 = (f32[2,512,512]{2,1,0:T(8,128)}, f32[2,512,512]{2,1,0:T(8,128)}, bf16[224,8,512]{2,1,0:T(8,128)(2,1)}, bf16[256,128]{1,0:T(8,128)(2,1)}) custom-call(s32[512]{0:T(512)} %max.12.src_ref, s32[128]{0:T(128)} %get-tuple-element.14.dense_ref, s32[128]{0:T(128)} %get-tuple-element.15.packed_ref, s32[224]{0:T(256)} %get-tuple-element.12.place_ref, ...), custom_call_target="tpu_custom_call" | custom-call | tf_op jit(solution)/shard_map/pallas_call | solution.py:367
  126.9 0.0 copy-start
  126.9 3.2 %copy.20 = f32[1,2,512,512]{3,2,1,0:T(8,128)} copy(f32[1,2,512,512]{3,2,1,0:T(8,128)} %bitcast.11) | data formatting | bytes 4194304
  130.1 0.0 copy-done
  130.1 0.0 copy-start.1
  130.1 1.3 copy.21
  131.5 0.9 copy-done.1
  132.4 0.0 copy-start.2
  132.4 1.2 copy.22
  133.6 0.0 copy-done.2
  133.6 0.6 copy.23
  (4 shorter events, 0.0 us)
Async XLA Ops:
  126.9 3.2 %copy-start = (f32[2,512,512]{2,1,0:T(8,128)S(1)}, f32[2,512,512]{2,1,0:T(8,128)}, u32[]{:S(2)}) copy-start(f32[2,512,512]{2,1,0:T(8,128)} %get-tuple-element.9) | copy-start | bytes 6291460
  130.1 2.3 %copy-start.1 = (bf16[224,8,512]{2,1,0:T(8,128)(2,1)S(1)}, bf16[224,8,512]{2,1,0:T(8,128)(2,1)}, u32[]{:S(2)}) copy-start(bf16[224,8,512]{2,1,0:T(8,128)(2,1)} %get-tuple-element.22) | copy-start | bytes 5505028
  132.4 1.2 copy-start.2

commit v4 on v3

v4 whole, which is shorter than its diff:
```python
import functools
import math

import jax
import jax.numpy as jnp
from jax import lax
from jax.experimental import pallas as pl
from jax.experimental.pallas import tpu as pltpu
from jax.sharding import PartitionSpec as P

BETA = 0.9
MESH = pl.DeviceIdType.MESH
VMEM = pltpu.VMEM
SMEM = pltpu.SMEM


def to_slab(rows):
    half = rows.shape[1] // 2
    return jnp.concatenate([rows[:, :half], rows[:, half:]], axis=0)


def from_slab(slab):
    half = slab.shape[0] // 2
    return jnp.concatenate([slab[:half], slab[half:]], axis=1)


def loop(count, body, unroll=1):
    def step(index, carry):
        body(index)
        return carry

    lax.fori_loop(0, count, step, 0, unroll=unroll)


class Place:
    def __init__(self, count):
        self.count = count
        self.pairs = count // 2
        self.deep, self.wide = (8, 4) if count == 64 else (count // 2, 1)
        self.replica = lax.axis_index("dp")
        self.me = lax.axis_index("mp")
        self.pair, self.core = self.me // 2, self.me % 2
        self.right = {"dp": lax.rem(self.replica + 1, 4)}
        self.left = {"dp": lax.rem(self.replica + 3, 4)}

    def partner(self, step):
        z, y = self.pair // self.wide, self.pair % self.wide
        z = lax.rem(z + lax.rem(step, self.deep) * 3, self.deep)
        y = lax.rem(y + step // self.deep, self.wide)
        return z * self.wide + y


CHUNKS = 4


def halves(cap):
    return pl.ds(0, cap // 2), pl.ds(cap // 2, cap - cap // 2)


def remote(src, dst, send_sem, recv_sem, device):
    return pltpu.make_async_remote_copy(
        src_ref=src, dst_ref=dst, send_sem=send_sem, recv_sem=recv_sem, device_id=device, device_id_type=MESH
    )


def greet(here):
    barrier = pltpu.get_barrier_semaphore()
    for device in (here.left, here.right, {"mp": here.pair * 2 + 1 - here.core}):
        pl.semaphore_signal(barrier, inc=1, device_id=device, device_id_type=MESH)

    def signal(step):
        for core in range(2):
            device = {"mp": here.partner(step + 1) * 2 + core}
            pl.semaphore_signal(barrier, inc=1, device_id=device, device_id_type=MESH)

    loop(here.pairs - 1, signal)
    pl.semaphore_wait(barrier, here.count + 1)


def hand_out(here, core, src, dst, send_sem, recv_sem):
    def send(pair):
        remote(src.at[pair], dst.at[here.me], send_sem, recv_sem, {"mp": pair * 2 + core}).start()

    @pl.when(here.core == core)
    def _():
        pltpu.make_async_copy(src.at[here.pair], dst.at[here.me], recv_sem).start()

    @pl.when(here.core != core)
    def _():
        send(here.pair)

    loop(here.pairs - 1, lambda step: send(here.partner(step + 1)))


def hand_back(here, src, dst, send_sem, recv_sem):
    def send(device):
        remote(src.at[device], dst.at[here.pair], send_sem, recv_sem, {"mp": device}).start()

    pltpu.make_async_copy(src.at[here.me], dst.at[here.pair], recv_sem).start()
    send(here.pair * 2 + 1 - here.core)

    def both(step):
        for core in range(2):
            send(here.partner(step + 1) * 2 + core)

    loop(here.pairs - 1, both)


def wait_all(ref, sem):
    pltpu.make_async_copy(ref, ref, sem).wait()


def scatter_copies(here, cap, buffers, send, recv):
    first, second = halves(cap)
    xs, tl, tr, fl, fr = buffers
    plan = (
        (xs.at[2, first], tl.at[first], here.right),
        (xs.at[2, second], tr.at[second], here.left),
        (xs.at[1, second], fl.at[second], here.right),
        (xs.at[3, first], fr.at[first], here.left),
        (xs.at[1, first], fl.at[first], here.right),
        (xs.at[3, second], fr.at[second], here.left),
    )
    return [remote(s, t, send.at[k], recv.at[k], to) for k, (s, t, to) in enumerate(plan)]


def gather_copies(here, cap, start, q, send, recv):
    first, second = (pl.ds(start + part.start, part.size) for part in halves(cap))
    plan = (
        (q.at[0, first], q.at[3, first], here.right),
        (q.at[0, second], q.at[1, second], here.left),
        (q.at[0, second], q.at[3, second], here.right),
        (q.at[0, first], q.at[1, first], here.left),
        (q.at[3, first], q.at[2, first], here.right),
        (q.at[1, second], q.at[2, second], here.left),
    )
    return [remote(s, t, send.at[k], recv.at[k], to) for k, (s, t, to) in enumerate(plan)]


LINEAR = -(5.0 / 16.0 + 3125.0 / 4096.0)
SQUARE = 3125.0 / 4096.0
CUBE = -1250.0 / 4096.0


def dot(left, right, dims=((1,), (0,))):
    return lax.dot_general(left, right, (dims, ((), ())), preferred_element_type=jnp.float32)


def column_parts(order, body):
    width = min(256, order)

    def one(part):
        body(pl.ds(pl.multiple_of(part * width, width), width))

    loop(order // width, one)


def excess(gram, result, first_b, second, second_b, third_b, tail_b, out):
    order = result.shape[0]

    def blend(columns):
        result[:, columns] = BETA * result[:, columns] + (1.0 - BETA) * gram(columns)

    column_parts(order, blend)
    whole = result[...]
    scale = 1.0 / jnp.sqrt(jnp.sum(whole * whole) + 1e-06)
    first_b[...] = (result[...] * scale).astype(jnp.bfloat16)

    def square(columns):
        value = dot(first_b[...], first_b[:, columns])
        second[:, columns] = value
        second_b[:, columns] = value.astype(jnp.bfloat16)

    column_parts(order, square)

    def cube(columns):
        third = dot(second_b[...], first_b[:, columns])
        first = result[:, columns] * scale
        two = second[:, columns]
        third_b[:, columns] = third.astype(jnp.bfloat16)
        tail_b[:, columns] = ((250.0 * first - 25.0 * two + third) * (1.0 / 4096.0)).astype(jnp.bfloat16)
        second[:, columns] = LINEAR * first + SQUARE * two + CUBE * third

    column_parts(order, cube)

    def last(columns):
        out[:, columns] = (second[:, columns] + dot(tail_b[...], third_b[:, columns])).astype(jnp.bfloat16)

    column_parts(order, last)


def attend(query, key, value, out):
    length, width = query.shape
    scores = dot(query[...], key[...], ((1,), (1,))) * (1.0 / math.sqrt(width))
    causal = lax.broadcasted_iota(jnp.int32, (length, length), 0) >= lax.broadcasted_iota(
        jnp.int32, (length, length), 1
    )
    scores = jnp.where(causal, scores, -jnp.inf)
    weights = jnp.exp(scores - jnp.max(scores, axis=-1, keepdims=True))
    probs = (weights / jnp.sum(weights, axis=-1, keepdims=True)).astype(jnp.bfloat16)
    out[...] = dot(probs, value[...]).astype(jnp.bfloat16)


def step_kernel(
    cap, count, table, query, key, value, grads_hbm, left_hbm, right_hbm,
    left_next, right_next, update_ref, attended,
    *scratch,
):
    buffers = [scratch[5 * chunk : 5 * chunk + 5] for chunk in range(CHUNKS)]
    rest = scratch[5 * CHUNKS :]
    out_slabs, in_slabs, out_back, in_back = rest[0:4], rest[4:6], rest[6:8], rest[8:12]
    grads_ref, stat_left, stat_right = rest[12:15]
    q, block, first_b, second, second_b, third_b, tail_b, left_b, right_b, half_b = rest[15:25]
    x_send, x_recv, g_send, g_recv, a_send, a_recv, b_send, b_recv, load, store = rest[25:]
    here = Place(count)
    pairs = here.pairs
    total = CHUNKS * cap
    first, last = halves(cap)

    loads = [
        pltpu.make_async_copy(source, target, load.at[k])
        for k, (source, target) in enumerate(
            ((grads_hbm, grads_ref), (left_hbm, stat_left), (right_hbm, stat_right))
        )
    ]
    for copy in loads:
        copy.start()
    greet(here)
    loads[0].wait()

    def pack(chunk, relative, part):
        base = lax.rem(here.replica + relative, 4) * total + chunk * cap + part.start
        xs = buffers[chunk][0]

        def one(index):
            number = table[0, base + index]
            xs[relative, part.start + index] = to_slab(grads_ref[number].astype(jnp.float32)).astype(jnp.bfloat16)

        loop(part.size, one, unroll=4)

    def add(chunk, relative, arrived, part):
        xs = buffers[chunk][0]

        def one(index):
            at = part.start + index
            both = xs[relative, at].astype(jnp.float32) + arrived[at].astype(jnp.float32)
            xs[relative, at] = both.astype(jnp.bfloat16)

        loop(part.size, one, unroll=4)

    reduce = [
        scatter_copies(here, cap, buffers[chunk], x_send.at[chunk], x_recv.at[chunk]) for chunk in range(CHUNKS)
    ]
    gather = [
        gather_copies(here, cap, chunk * cap, q, g_send.at[chunk], g_recv.at[chunk]) for chunk in range(CHUNKS)
    ]

    def open_chunk(chunk):
        for relative, part, copy in ((2, first, 0), (2, last, 1), (1, last, 2), (3, first, 3)):
            pack(chunk, relative, part)
            reduce[chunk][copy].start()
        for relative, part in ((1, first), (3, last), (0, first), (0, last)):
            pack(chunk, relative, part)

    def relay(chunk):
        reduce[chunk][0].wait_recv()
        add(chunk, 1, buffers[chunk][1], first)
        reduce[chunk][4].start()
        reduce[chunk][1].wait_recv()
        add(chunk, 3, buffers[chunk][2], last)
        reduce[chunk][5].start()

    def finish(chunk):
        for copy in range(2, 6):
            reduce[chunk][copy].wait_recv()
        xs, _, _, fl, fr = buffers[chunk]

        def one(owner):
            place = table[1, here.replica * (CHUNKS * pairs) + chunk * pairs + owner]
            at = jnp.maximum(place, 0)
            whole = xs[0, at].astype(jnp.float32) + fl[at].astype(jnp.float32) + fr[at].astype(jnp.float32)
            out_slabs[chunk][owner] = jnp.where(place >= 0, whole, 0.0).astype(jnp.bfloat16)

        loop(pairs, one, unroll=4)
        slot = chunk // 2
        hand_out(here, chunk % 2, out_slabs[chunk], in_slabs[slot], a_send.at[slot], a_recv.at[slot])

    def stored(slot, side):
        source, target = ((stat_left, left_next), (stat_right, right_next))[side]
        return pltpu.make_async_copy(source.at[slot], target.at[slot], store.at[slot, side])

    def precondition(slot):
        wait_all(in_slabs[slot], a_recv.at[slot])

        def place(pair):
            upper = from_slab(in_slabs[slot][2 * pair].astype(jnp.float32))
            lower = from_slab(in_slabs[slot][2 * pair + 1].astype(jnp.float32))
            rows = pl.ds(pl.multiple_of(pair * 16, 16), 16)
            block[rows] = jnp.concatenate([upper, lower], axis=0).astype(jnp.bfloat16)

        loop(count // 2, place, unroll=2)
        order = block.shape[0]
        spare = (first_b, second, second_b, third_b, tail_b)
        excess(
            lambda columns: dot(block[...], block[columns], ((1,), (1,))), stat_left.at[slot], *spare, left_b
        )
        stored(slot, 0).start()
        excess(
            lambda columns: dot(block[...], block[:, columns], ((0,), (0,))), stat_right.at[slot], *spare, right_b
        )
        stored(slot, 1).start()

        def left_side(columns):
            part = (25.0 / 16.0) * block[:, columns].astype(jnp.float32) + dot(left_b[...], block[:, columns])
            second[:, columns] = part
            half_b[:, columns] = part.astype(jnp.bfloat16)

        column_parts(order, left_side)

        def right_side(columns):
            second[:, columns] = (25.0 / 16.0) * second[:, columns] + dot(half_b[...], right_b[:, columns])

        column_parts(order, right_side)
        raw = second[...]
        widened = block[...].astype(jnp.float32)
        mean_raw = jnp.sum(raw * raw) * (1.0 / raw.size)
        mean_block = jnp.sum(widened * widened) * (1.0 / raw.size)
        scale = jnp.sqrt((mean_block + 1e-06) / (mean_raw + 1e-06))

        def cut(owner):
            rows = pl.ds(pl.multiple_of(owner * 8, 8), 8)
            out_back[slot][owner] = to_slab(second[rows] * scale).astype(jnp.bfloat16)

        loop(count, cut, unroll=4)
        for core in range(2):

            @pl.when(here.core == core)
            def _():
                chunk = slot * 2 + core
                hand_back(here, out_back[slot], in_back[chunk], b_send.at[slot], b_recv.at[chunk])

    def open_gather(chunk):
        wait_all(in_back[chunk], b_recv.at[chunk])
        for part, starts in ((first, (0, 3)), (last, (1, 2))):

            def one(index):
                at = chunk * cap + part.start + index
                q[0, at] = in_back[chunk][table[2, at]]

            loop(part.size, one, unroll=4)
            for copy in starts:
                gather[chunk][copy].start()

    def forward(chunk):
        for arrived, onward in ((0, 4), (1, 5)):
            gather[chunk][arrived].wait_recv()
            gather[chunk][onward].start()

    open_chunk(0)
    attend(query, key, value, attended)
    for chunk in range(CHUNKS):
        relay(chunk)
        if chunk + 1 < CHUNKS:
            open_chunk(chunk + 1)
        finish(chunk)
    loads[1].wait()
    loads[2].wait()
    precondition(0)
    precondition(1)
    for chunk in range(CHUNKS):
        open_gather(chunk)
        forward(chunk)
    for chunk in range(CHUNKS):
        for copy in range(2, 6):
            gather[chunk][copy].wait_recv()

    def settle(number):
        place = table[3, number]
        slab = q[place // total, place % total]
        update_ref[number] = from_slab(slab.astype(jnp.float32)).astype(jnp.bfloat16)

    loop(update_ref.shape[0], settle, unroll=8)
    for chunk in range(CHUNKS):
        for copy in reduce[chunk] + gather[chunk]:
            copy.wait_send()
    for slot in range(2):
        wait_all(out_back[slot].at[pl.ds(0, count - 1)], a_send.at[slot])
        wait_all(out_back[slot].at[pl.ds(0, count - 1)], b_send.at[slot])
        for side in range(2):
            stored(slot, side).wait()


def step(grads, stat_left, stat_right, query, key, value, table, cap, count, number):
    blocks, rows, columns = grads.shape
    order = stat_left.shape[1]
    slab = (2 * rows, columns // 2)
    narrow = VMEM((order, order), jnp.bfloat16)
    wide = VMEM((order, order), jnp.float32)
    some = VMEM((count // 2,) + slab, jnp.bfloat16)
    every = VMEM((count,) + slab, jnp.bfloat16)
    dma = pltpu.SemaphoreType.DMA
    near, far = pl.BlockSpec(memory_space=VMEM), pl.BlockSpec(memory_space=pl.ANY)
    return pl.pallas_call(
        functools.partial(step_kernel, cap, count),
        out_shape=(
            jax.ShapeDtypeStruct(stat_left.shape, jnp.float32),
            jax.ShapeDtypeStruct(stat_right.shape, jnp.float32),
            jax.ShapeDtypeStruct(grads.shape, jnp.bfloat16),
            jax.ShapeDtypeStruct(query.shape, jnp.bfloat16),
        ),
        in_specs=[pl.BlockSpec(memory_space=SMEM), near, near, near, far, far, far],
        out_specs=[far, far, near, near],
        scratch_shapes=[
            *[
                VMEM(lead + slab, jnp.bfloat16)
                for chunk in range(CHUNKS)
                for lead in ((4, cap), (cap,), (cap,), (cap,), (cap,))
            ],
            *[some] * 4, *[every] * 2, *[every] * 2, *[some] * 4,
            VMEM(grads.shape, jnp.bfloat16), VMEM(stat_left.shape, jnp.float32), VMEM(stat_left.shape, jnp.float32),
            VMEM((4, CHUNKS * cap) + slab, jnp.bfloat16),
            narrow, narrow, wide, narrow, narrow, narrow, narrow, narrow, narrow,
            dma((CHUNKS, 6)), dma((CHUNKS, 6)), dma((CHUNKS, 6)), dma((CHUNKS, 6)),
            dma((2,)), dma((2,)), dma((2,)), dma((CHUNKS,)), dma((3,)), dma((2, 2)),
        ],
        compiler_params=pltpu.CompilerParams(
            collective_id=number, has_side_effects=True, vmem_limit_bytes=56 * 2**20
        ),
    )(table, query, key, value, grads, stat_left, stat_right)


def table_kernel(cap, count, assign_ref, table):
    blocks = assign_ref.shape[1]
    pairs = count // 2
    slots = 8 * count
    width = table.shape[1]
    here = lax.axis_index("dp")
    wide = lax.broadcast_in_dim(assign_ref[...], (width, blocks), (0, 1))
    slot = wide.T
    number = lax.broadcasted_iota(jnp.int32, (blocks, width), 0)
    lane = lax.broadcasted_iota(jnp.int32, (blocks, width), 1)
    inside = lane % pairs
    chunk = (lane // pairs) % CHUNKS
    replica = lane // (CHUNKS * pairs)
    listed = replica * (CHUNKS * pairs) + 4 * inside + 2 * (chunk % 2) + chunk // 2
    hit = jnp.where(slot == listed, 1.0, 0.0)
    taken = jnp.sum(hit, axis=0, keepdims=True)
    before = lax.broadcasted_iota(jnp.int32, (width, width), 0)
    after = lax.broadcasted_iota(jnp.int32, (width, width), 1)
    counts = jnp.where((before < after) & (before // pairs == after // pairs), 1.0, 0.0).astype(jnp.bfloat16)
    rank = dot(lax.broadcast_in_dim(taken, (8, width), (0, 1)).astype(jnp.bfloat16), counts)[0:1]
    own_rank = jnp.sum(hit * rank, axis=1, keepdims=True).astype(jnp.int32)
    own_chunk = 2 * (slot % 2) + (slot // 2) % 2
    own_replica = slot // (CHUNKS * pairs)
    packed = own_chunk * cap + own_rank
    place = own_replica * (CHUNKS * cap) + packed
    table[...] = jnp.zeros(table.shape, jnp.int32)
    table[0:1] = jnp.sum(jnp.where(place == lane, number, 0), axis=0, keepdims=True)
    table[1:2] = jnp.where(taken > 0.0, rank.astype(jnp.int32), -1)
    owner = (slot // 4) % pairs
    table[2:3] = jnp.sum(jnp.where(place == lane + here * (CHUNKS * cap), owner, 0), axis=0, keepdims=True)
    relative = (own_replica - here + 4) % 4
    found = relative * (CHUNKS * cap) + packed
    table[3:4, 0:blocks] = found.T[0:1]
    most = jnp.max(own_rank + 1)
    table[4:5] = jnp.full((1, width), most, jnp.int32)


def make_table(assign, cap, count):
    width = 8 * count
    return pl.pallas_call(
        functools.partial(table_kernel, cap, count),
        out_shape=jax.ShapeDtypeStruct((8, width), jnp.int32),
        in_specs=[pl.BlockSpec(memory_space=VMEM)],
        out_specs=pl.BlockSpec(memory_space=VMEM),
        compiler_params=pltpu.CompilerParams(vmem_limit_bytes=32 * 2**20),
    )(assign.reshape(1, -1))


def body(partial_grads, stat_left, stat_right, assign, query_vectors, key_vectors, value_vectors):
    count = lax.axis_size("mp")
    full = count // 2
    cap = 3 * full // 4
    arrays = (
        partial_grads[0], stat_left[0], stat_right[0], query_vectors, key_vectors, value_vectors,
    )
    table = make_table(assign, cap, count)
    left_next, right_next, update, attended = lax.cond(
        table[4, 0] <= cap,
        lambda: step(*arrays, table, cap, count, 0),
        lambda: step(*arrays, make_table(assign, full, count), full, count, 1),
    )
    return (left_next[None], right_next[None], update, attended)


def solution(mesh):
    placed = (
        P("dp", None, "mp", None),
        P("dp", "mp", None, None),
        P("dp", "mp", None, None),
        P(),
        P("dp", "mp"),
        P("dp", "mp"),
        P("dp", "mp"),
    )
    return jax.shard_map(
        body,
        mesh=mesh,
        in_specs=placed,
        out_specs=(
            P("dp", "mp", None, None),
            P("dp", "mp", None, None),
            P(None, "mp", None),
            P("dp", "mp"),
        ),
        check_vma=False,
    )
```

time: 134 us -> 109 us (0.81); the launches traced: 134 us -> 107 us
  Pallas kernels: 122 us -> 101 us
  local copies, waits for them, and re-layouts: 9.63 us -> 5.01 us
  other arithmetic: 1.8 us -> 0 us
    pallas_call x1 -> x2, Pallas kernels: 122 us -> 101 us  [the longest x1 99.4 us: step(): pl.pallas_call(functools.partial(step_kernel, cap, count), out_shape=(jax...]
    unnamed x10 -> x4, local copies, waits for them, and re-layouts: 7.35 us -> 4.5 us
where the time goes in v4:
time: 109 us; the launch traced here: 107 us
  Pallas kernels  101 us (93%)
  local copies, waits for them, and re-layouts  5.01 us (5%)
  between operations  1.29 us (1%)
    pallas_call x1, Pallas kernels, step(): pl.pallas_call(functools.partial(step_kernel, cap, count), out_shape=(jax...  99.4 us
    unnamed x4, local copies, waits for them, and re-layouts  4.5 us

profile of v4, /device:TPU:2, one launch (start us, length us, event | category | flops | bytes accessed | tf_op | source)
XLA Modules:
  0.0 107.4 jit_solution(1017426934643106089)
XLA Ops:
  0.6 1.4 %shard_map.102 = s32[8,512]{1,0:T(8,128)S(1)} custom-call(s32[1,224]{1,0:T(1,128)} %bitcast.16), custom_call_target="tpu_custom_call" | custom-call | tf_op jit(solution)/shard_map/pallas_call | solution.py:471
  2.0 0.5 slice.4
  3.2 99.7 %conditional.1 = ((f32[2,512,512]{2,1,0:T(8,128)S(1)}, f32[2,512,512]{2,1,0:T(8,128)S(1)}, bf16[224,8,512]{2,1,0:T(8,128)(2,1)S(1)}, bf16[256,128]{1,0:T(8,128)(2,1)S(1)})) conditional(s32[]{:T(128)} %bitcast.2, (s32[224]{0:T(256)}, bf16[256,128]{1,0:T(8,128)(2,1)}, bf16[256,128]{1,0:T(8,128)(2,1)}, bf16[256,128]{1,0:T(8,128)(2,1)}, ...), branch_computations={%region_0.0_spmd, %region_1.0_spmd} | conditional | bytes 65572 | solution.py:488
  3.2 99.4 %branch_1_fun.1 = (f32[2,512,512]{2,1,0:T(8,128)S(1)}, f32[2,512,512]{2,1,0:T(8,128)S(1)}, bf16[224,8,512]{2,1,0:T(8,128)(2,1)S(1)}, bf16[256,128]{1,0:T(8,128)(2,1)S(1)}) custom-call(s32[8,512]{1,0:T(8,128)S(1)} %get-tuple-element.50.table, bf16[256,128]{1,0:T(8,128)(2,1)} %get-tuple-element.51.query, bf16[256,128]{1,0:T(8,128)(2,1)} %get-tuple-element.52.key, ...), custom_call_target="tpu_custom_call" | custom-call | tf_op jit(solution)/shard_map/cond/branch_1_fun/pallas_call | solution.py:403
  102.9 1.3 %copy.23 = f32[1,2,512,512]{3,2,1,0:T(8,128)} copy(f32[1,2,512,512]{3,2,1,0:T(8,128)S(1)} %bitcast.14) | data formatting | bytes 4194304
  104.2 1.3 %copy.24 = f32[1,2,512,512]{3,2,1,0:T(8,128)} copy(f32[1,2,512,512]{3,2,1,0:T(8,128)S(1)} %bitcast.15) | data formatting | bytes 4194304
  105.5 1.2 %copy.25 = bf16[224,8,512]{2,1,0:T(8,128)(2,1)} copy(bf16[224,8,512]{2,1,0:T(8,128)(2,1)S(1)} %get-tuple-element.100) | data formatting | bytes 3670016
  106.7 0.6 copy.26

commit v5 on v4

--- a/solution.py
+++ b/solution.py
@@ -43,14 +43,25 @@
         self.right = {"dp": lax.rem(self.replica + 1, 4)}
         self.left = {"dp": lax.rem(self.replica + 3, 4)}
 
-    def partner(self, step):
+    def visit(self, send, cores=(0, 1)):
         z, y = self.pair // self.wide, self.pair % self.wide
-        z = lax.rem(z + lax.rem(step, self.deep) * 3, self.deep)
-        y = lax.rem(y + step // self.deep, self.wide)
-        return z * self.wide + y
+        rows = [y] + [lax.rem(y + step, self.wide) for step in range(1, self.wide)]
+
+        def turn(step):
+            away = self.deep // 2 + (1 - 2 * (step % 2)) * ((step + 1) // 2)
+            base = lax.rem(z + away, self.deep) * self.wide
+            for row in rows:
+                for core in cores:
+                    send(base + row, core)
+
+        loop(self.deep - 1, turn)
+        for row in rows[1:]:
+            for core in cores:
+                send(z * self.wide + row, core)
 
 
 CHUNKS = 4
+PARTS = 4
 
 
 def halves(cap):
@@ -68,17 +79,14 @@
     for device in (here.left, here.right, {"mp": here.pair * 2 + 1 - here.core}):
         pl.semaphore_signal(barrier, inc=1, device_id=device, device_id_type=MESH)
 
-    def signal(step):
-        for core in range(2):
-            device = {"mp": here.partner(step + 1) * 2 + core}
-            pl.semaphore_signal(barrier, inc=1, device_id=device, device_id_type=MESH)
-
-    loop(here.pairs - 1, signal)
-    pl.semaphore_wait(barrier, here.count + 1)
+    def signal(pair, core):
+        pl.semaphore_signal(barrier, inc=1, device_id={"mp": pair * 2 + core}, device_id_type=MESH)
+
+    here.visit(signal)
 
 
 def hand_out(here, core, src, dst, send_sem, recv_sem):
-    def send(pair):
+    def send(pair, core):
         remote(src.at[pair], dst.at[here.me], send_sem, recv_sem, {"mp": pair * 2 + core}).start()
 
     @pl.when(here.core == core)
@@ -87,23 +95,19 @@
 
     @pl.when(here.core != core)
     def _():
-        send(here.pair)
-
-    loop(here.pairs - 1, lambda step: send(here.partner(step + 1)))
+        send(here.pair, core)
+
+    here.visit(send, (core,))
 
 
 def hand_back(here, src, dst, send_sem, recv_sem):
-    def send(device):
-        remote(src.at[device], dst.at[here.pair], send_sem, recv_sem, {"mp": device}).start()
-
-    pltpu.make_async_copy(src.at[here.me], dst.at[here.pair], recv_sem).start()
-    send(here.pair * 2 + 1 - here.core)
-
-    def both(step):
-        for core in range(2):
-            send(here.partner(step + 1) * 2 + core)
-
-    loop(here.pairs - 1, both)
+    def send(pair, core):
+        device = pair * 2 + core
+        remote(src.at[device], dst.at[here.me], send_sem, recv_sem, {"mp": device}).start()
+
+    pltpu.make_async_copy(src.at[here.me], dst.at[here.me], recv_sem).start()
+    send(here.pair, 1 - here.core)
+    here.visit(send)
 
 
 def wait_all(ref, sem):
@@ -124,8 +128,8 @@
     return [remote(s, t, send.at[k], recv.at[k], to) for k, (s, t, to) in enumerate(plan)]
 
 
-def gather_copies(here, cap, start, q, send, recv):
-    first, second = (pl.ds(start + part.start, part.size) for part in halves(cap))
+def gather_copies(here, cap, q, send, recv):
+    first, second = halves(cap)
     plan = (
         (q.at[0, first], q.at[3, first], here.right),
         (q.at[0, second], q.at[1, second], here.left),
@@ -202,20 +206,21 @@
 
 
 def step_kernel(
-    cap, count, table, query, key, value, grads_hbm, left_hbm, right_hbm,
+    bounds, back_cap, count, table, query, key, value, grads_hbm, left_hbm, right_hbm,
     left_next, right_next, update_ref, attended,
     *scratch,
 ):
     buffers = [scratch[5 * chunk : 5 * chunk + 5] for chunk in range(CHUNKS)]
     rest = scratch[5 * CHUNKS :]
-    out_slabs, in_slabs, out_back, in_back = rest[0:4], rest[4:6], rest[6:8], rest[8:12]
-    grads_ref, stat_left, stat_right = rest[12:15]
-    q, block, first_b, second, second_b, third_b, tail_b, left_b, right_b, half_b = rest[15:25]
-    x_send, x_recv, g_send, g_recv, a_send, a_recv, b_send, b_recv, load, store = rest[25:]
+    out_slabs, in_slabs, out_back, in_back, q = rest[0:4], rest[4:6], rest[6:10], rest[10:14], rest[14:18]
+    summed, grads_ref, stat_left, stat_right = rest[18:22]
+    block, first_b, second, second_b, third_b, tail_b, left_b, right_b, half_b = rest[22:31]
+    x_send, x_recv, g_send, g_recv, a_send, a_recv, b_send, b_recv, load, store = rest[31:]
     here = Place(count)
     pairs = here.pairs
-    total = CHUNKS * cap
-    first, last = halves(cap)
+    total = bounds[-1]
+    begins = (0,) + bounds[:-1]
+    caps = [end - begin for begin, end in zip(begins, bounds)]
 
     loads = [
         pltpu.make_async_copy(source, target, load.at[k])
@@ -229,7 +234,7 @@
     loads[0].wait()
 
     def pack(chunk, relative, part):
-        base = lax.rem(here.replica + relative, 4) * total + chunk * cap + part.start
+        base = lax.rem(here.replica + relative, 4) * total + begins[chunk] + part.start
         xs = buffers[chunk][0]
 
         def one(index):
@@ -249,20 +254,27 @@
         loop(part.size, one, unroll=4)
 
     reduce = [
-        scatter_copies(here, cap, buffers[chunk], x_send.at[chunk], x_recv.at[chunk]) for chunk in range(CHUNKS)
+        scatter_copies(here, caps[chunk], buffers[chunk], x_send.at[chunk], x_recv.at[chunk]) for chunk in range(CHUNKS)
     ]
     gather = [
-        gather_copies(here, cap, chunk * cap, q, g_send.at[chunk], g_recv.at[chunk]) for chunk in range(CHUNKS)
+        gather_copies(here, back_cap, q[part], g_send.at[part], g_recv.at[part]) for part in range(PARTS)
     ]
 
     def open_chunk(chunk):
+        first, last = halves(caps[chunk])
         for relative, part, copy in ((2, first, 0), (2, last, 1), (1, last, 2), (3, first, 3)):
             pack(chunk, relative, part)
-            reduce[chunk][copy].start()
+            if chunk > 0:
+                reduce[chunk][copy].start()
         for relative, part in ((1, first), (3, last), (0, first), (0, last)):
             pack(chunk, relative, part)
+        if chunk == 0:
+            pl.semaphore_wait(pltpu.get_barrier_semaphore(), here.count + 1)
+            for copy in range(4):
+                reduce[chunk][copy].start()
 
     def relay(chunk):
+        first, last = halves(caps[chunk])
         reduce[chunk][0].wait_recv()
         add(chunk, 1, buffers[chunk][1], first)
         reduce[chunk][4].start()
@@ -275,10 +287,15 @@
             reduce[chunk][copy].wait_recv()
         xs, _, _, fl, fr = buffers[chunk]
 
+        def gather_up(index):
+            whole = xs[0, index].astype(jnp.float32) + fl[index].astype(jnp.float32) + fr[index].astype(jnp.float32)
+            summed[begins[chunk] + index] = whole.astype(jnp.bfloat16)
+
+        loop(caps[chunk], gather_up, unroll=4)
+
         def one(owner):
             place = table[1, here.replica * (CHUNKS * pairs) + chunk * pairs + owner]
-            at = jnp.maximum(place, 0)
-            whole = xs[0, at].astype(jnp.float32) + fl[at].astype(jnp.float32) + fr[at].astype(jnp.float32)
+            whole = summed[jnp.maximum(place, 0)].astype(jnp.float32)
             out_slabs[chunk][owner] = jnp.where(place >= 0, whole, 0.0).astype(jnp.bfloat16)
 
         loop(pairs, one, unroll=4)
@@ -289,7 +306,9 @@
         source, target = ((stat_left, left_next), (stat_right, right_next))[side]
         return pltpu.make_async_copy(source.at[slot], target.at[slot], store.at[slot, side])
 
-    def precondition(slot):
+    spare = (first_b, second, second_b, third_b, tail_b)
+
+    def left_root(slot):
         wait_all(in_slabs[slot], a_recv.at[slot])
 
         def place(pair):
@@ -299,16 +318,19 @@
             block[rows] = jnp.concatenate([upper, lower], axis=0).astype(jnp.bfloat16)
 
         loop(count // 2, place, unroll=2)
-        order = block.shape[0]
-        spare = (first_b, second, second_b, third_b, tail_b)
         excess(
             lambda columns: dot(block[...], block[columns], ((1,), (1,))), stat_left.at[slot], *spare, left_b
         )
         stored(slot, 0).start()
+
+    def right_root(slot):
         excess(
             lambda columns: dot(block[...], block[:, columns], ((0,), (0,))), stat_right.at[slot], *spare, right_b
         )
         stored(slot, 1).start()
+
+    def precondition(slot):
+        order = block.shape[0]
 
         def left_side(columns):
             part = (25.0 / 16.0) * block[:, columns].astype(jnp.float32) + dot(left_b[...], block[:, columns])
@@ -329,27 +351,28 @@
 
         def cut(owner):
             rows = pl.ds(pl.multiple_of(owner * 8, 8), 8)
-            out_back[slot][owner] = to_slab(second[rows] * scale).astype(jnp.bfloat16)
+            ready = to_slab(second[rows] * scale).astype(jnp.bfloat16)
+            width = ready.shape[1] // 2
+            out_back[2 * slot][owner] = ready[:, :width]
+            out_back[2 * slot + 1][owner] = ready[:, width:]
 
         loop(count, cut, unroll=4)
-        for core in range(2):
-
-            @pl.when(here.core == core)
-            def _():
-                chunk = slot * 2 + core
-                hand_back(here, out_back[slot], in_back[chunk], b_send.at[slot], b_recv.at[chunk])
-
-    def open_gather(chunk):
-        wait_all(in_back[chunk], b_recv.at[chunk])
-        for part, starts in ((first, (0, 3)), (last, (1, 2))):
+
+    def send_back(part):
+        hand_back(here, out_back[part], in_back[part], b_send.at[part], b_recv.at[part])
+
+    def open_gather(part):
+        wait_all(in_back[part], b_recv.at[part])
+        base = part // 2 * back_cap
+        for half, starts in zip(halves(back_cap), ((0, 3), (1, 2))):
 
             def one(index):
-                at = chunk * cap + part.start + index
-                q[0, at] = in_back[chunk][table[2, at]]
-
-            loop(part.size, one, unroll=4)
+                at = half.start + index
+                q[part][0, at] = in_back[part][table[2, base + at]]
+
+            loop(half.size, one, unroll=4)
             for copy in starts:
-                gather[chunk][copy].start()
+                gather[part][copy].start()
 
     def forward(chunk):
         for arrived, onward in ((0, 4), (1, 5)):
@@ -362,46 +385,63 @@
         relay(chunk)
         if chunk + 1 < CHUNKS:
             open_chunk(chunk + 1)
+        else:
+            loads[1].wait()
+            loads[2].wait()
+            left_root(0)
         finish(chunk)
-    loads[1].wait()
-    loads[2].wait()
+    right_root(0)
     precondition(0)
+    send_back(0)
+    send_back(1)
+    left_root(1)
+    right_root(1)
+    open_gather(0)
     precondition(1)
-    for chunk in range(CHUNKS):
-        open_gather(chunk)
-        forward(chunk)
-    for chunk in range(CHUNKS):
+    send_back(2)
+    forward(0)
+    send_back(3)
+    for part in range(1, PARTS):
+        open_gather(part)
+        forward(part)
+    for part in range(PARTS):
         for copy in range(2, 6):
-            gather[chunk][copy].wait_recv()
+            gather[part][copy].wait_recv()
 
     def settle(number):
         place = table[3, number]
-        slab = q[place // total, place % total]
-        update_ref[number] = from_slab(slab.astype(jnp.float32)).astype(jnp.bfloat16)
+        slot, inside = place // (4 * back_cap), place % (4 * back_cap)
+        relative, at = inside // back_cap, inside % back_cap
+        pieces = [q[part][relative, at].astype(jnp.float32) for part in range(PARTS)]
+        sides = [jnp.where(slot == 0, pieces[side], pieces[2 + side]) for side in range(2)]
+        slab = jnp.concatenate(sides, axis=1)
+        update_ref[number] = from_slab(slab).astype(jnp.bfloat16)
 
     loop(update_ref.shape[0], settle, unroll=8)
-    for chunk in range(CHUNKS):
-        for copy in reduce[chunk] + gather[chunk]:
+    for copies in reduce + gather:
+        for copy in copies:
             copy.wait_send()
     for slot in range(2):
-        wait_all(out_back[slot].at[pl.ds(0, count - 1)], a_send.at[slot])
-        wait_all(out_back[slot].at[pl.ds(0, count - 1)], b_send.at[slot])
+        wait_all(in_slabs[slot].at[pl.ds(0, count - 1)], a_send.at[slot])
         for side in range(2):
             stored(slot, side).wait()
-
-
-def step(grads, stat_left, stat_right, query, key, value, table, cap, count, number):
+    for part in range(PARTS):
+        wait_all(out_back[part].at[pl.ds(0, count - 1)], b_send.at[part])
+
+
+def step(grads, stat_left, stat_right, query, key, value, table, bounds, back_cap, count, number):
     blocks, rows, columns = grads.shape
     order = stat_left.shape[1]
-    slab = (2 * rows, columns // 2)
+    slab, thin = (2 * rows, columns // 2), (2 * rows, columns // 4)
     narrow = VMEM((order, order), jnp.bfloat16)
     wide = VMEM((order, order), jnp.float32)
     some = VMEM((count // 2,) + slab, jnp.bfloat16)
     every = VMEM((count,) + slab, jnp.bfloat16)
+    slim = VMEM((count,) + thin, jnp.bfloat16)
     dma = pltpu.SemaphoreType.DMA
     near, far = pl.BlockSpec(memory_space=VMEM), pl.BlockSpec(memory_space=pl.ANY)
     return pl.pallas_call(
-        functools.partial(step_kernel, cap, count),
+        functools.partial(step_kernel, bounds, back_cap, count),
         out_shape=(
             jax.ShapeDtypeStruct(stat_left.shape, jnp.float32),
             jax.ShapeDtypeStruct(stat_right.shape, jnp.float32),
@@ -413,15 +453,16 @@
         scratch_shapes=[
             *[
                 VMEM(lead + slab, jnp.bfloat16)
-                for chunk in range(CHUNKS)
+                for cap in [end - begin for begin, end in zip((0,) + bounds, bounds)]
                 for lead in ((4, cap), (cap,), (cap,), (cap,), (cap,))
             ],
-            *[some] * 4, *[every] * 2, *[every] * 2, *[some] * 4,
+            *[some] * 4, *[every] * 2, *[slim] * (2 * PARTS),
+            *[VMEM((4, back_cap) + thin, jnp.bfloat16)] * PARTS,
+            VMEM((bounds[-1],) + slab, jnp.bfloat16),
             VMEM(grads.shape, jnp.bfloat16), VMEM(stat_left.shape, jnp.float32), VMEM(stat_left.shape, jnp.float32),
-            VMEM((4, CHUNKS * cap) + slab, jnp.bfloat16),
             narrow, narrow, wide, narrow, narrow, narrow, narrow, narrow, narrow,
-            dma((CHUNKS, 6)), dma((CHUNKS, 6)), dma((CHUNKS, 6)), dma((CHUNKS, 6)),
-            dma((2,)), dma((2,)), dma((2,)), dma((CHUNKS,)), dma((3,)), dma((2, 2)),
+            dma((CHUNKS, 6)), dma((CHUNKS, 6)), dma((PARTS, 6)), dma((PARTS, 6)),
+            dma((2,)), dma((2,)), dma((PARTS,)), dma((PARTS,)), dma((3,)), dma((2, 2)),
         ],
         compiler_params=pltpu.CompilerParams(
             collective_id=number, has_side_effects=True, vmem_limit_bytes=56 * 2**20
@@ -429,7 +470,7 @@
     )(table, query, key, value, grads, stat_left, stat_right)
 
 
-def table_kernel(cap, count, assign_ref, table):
+def table_kernel(bounds, back_cap, count, assign_ref, table, over):
     blocks = assign_ref.shape[1]
     pairs = count // 2
     slots = 8 * count
@@ -447,48 +488,58 @@
     taken = jnp.sum(hit, axis=0, keepdims=True)
     before = lax.broadcasted_iota(jnp.int32, (width, width), 0)
     after = lax.broadcasted_iota(jnp.int32, (width, width), 1)
-    counts = jnp.where((before < after) & (before // pairs == after // pairs), 1.0, 0.0).astype(jnp.bfloat16)
-    rank = dot(lax.broadcast_in_dim(taken, (8, width), (0, 1)).astype(jnp.bfloat16), counts)[0:1]
-    own_rank = jnp.sum(hit * rank, axis=1, keepdims=True).astype(jnp.int32)
+    taken_b = lax.broadcast_in_dim(taken, (8, width), (0, 1)).astype(jnp.bfloat16)
+
+    def ranks(group):
+        counts = jnp.where((before < after) & (before // group == after // group), 1.0, 0.0).astype(jnp.bfloat16)
+        rank = dot(taken_b, counts)[0:1]
+        return rank, jnp.sum(hit * rank, axis=1, keepdims=True).astype(jnp.int32)
+
+    rank, own_rank = ranks(CHUNKS * pairs)
+    _, back_rank = ranks(2 * pairs)
     own_chunk = 2 * (slot % 2) + (slot // 2) % 2
     own_replica = slot // (CHUNKS * pairs)
-    packed = own_chunk * cap + own_rank
-    place = own_replica * (CHUNKS * cap) + packed
+    place = own_replica * bounds[-1] + own_rank
+    bound = jnp.full(own_chunk.shape, bounds[0], jnp.int32)
+    for chunk_number in range(1, CHUNKS):
+        bound = jnp.where(own_chunk == chunk_number, bounds[chunk_number], bound)
     table[...] = jnp.zeros(table.shape, jnp.int32)
     table[0:1] = jnp.sum(jnp.where(place == lane, number, 0), axis=0, keepdims=True)
     table[1:2] = jnp.where(taken > 0.0, rank.astype(jnp.int32), -1)
-    owner = (slot // 4) % pairs
-    table[2:3] = jnp.sum(jnp.where(place == lane + here * (CHUNKS * cap), owner, 0), axis=0, keepdims=True)
+    owner = (slot // 2) % count
+    back = (slot % 2) * back_cap + back_rank
+    mine = jnp.where(own_replica == here, back, -1)
+    table[2:3] = jnp.sum(jnp.where(mine == lane, owner, 0), axis=0, keepdims=True)
     relative = (own_replica - here + 4) % 4
-    found = relative * (CHUNKS * cap) + packed
+    found = (slot % 2) * (4 * back_cap) + relative * back_cap + back_rank
     table[3:4, 0:blocks] = found.T[0:1]
-    most = jnp.max(own_rank + 1)
-    table[4:5] = jnp.full((1, width), most, jnp.int32)
-
-
-def make_table(assign, cap, count):
+    over[0, 0] = jnp.maximum(jnp.max(own_rank - bound), jnp.max(back_rank) - back_cap) + 1
+
+
+def make_table(assign, bounds, back_cap, count):
     width = 8 * count
     return pl.pallas_call(
-        functools.partial(table_kernel, cap, count),
-        out_shape=jax.ShapeDtypeStruct((8, width), jnp.int32),
+        functools.partial(table_kernel, bounds, back_cap, count),
+        out_shape=(jax.ShapeDtypeStruct((8, width), jnp.int32), jax.ShapeDtypeStruct((1, 1), jnp.int32)),
         in_specs=[pl.BlockSpec(memory_space=VMEM)],
-        out_specs=pl.BlockSpec(memory_space=VMEM),
+        out_specs=(pl.BlockSpec(memory_space=VMEM), pl.BlockSpec(memory_space=SMEM)),
         compiler_params=pltpu.CompilerParams(vmem_limit_bytes=32 * 2**20),
     )(assign.reshape(1, -1))
 
 
 def body(partial_grads, stat_left, stat_right, assign, query_vectors, key_vectors, value_vectors):
     count = lax.axis_size("mp")
-    full = count // 2
-    cap = 3 * full // 4
     arrays = (
         partial_grads[0], stat_left[0], stat_right[0], query_vectors, key_vectors, value_vectors,
     )
-    table = make_table(assign, cap, count)
+    pairs = count // 2
+    tight = tuple(pairs * part // 4 for part in (3, 5, 7, 9)), 5 * count // 8
+    full = tuple(pairs * part for part in (1, 2, 3, 4)), count
+    table, over = make_table(assign, *tight, count)
     left_next, right_next, update, attended = lax.cond(
-        table[4, 0] <= cap,
-        lambda: step(*arrays, table, cap, count, 0),
-        lambda: step(*arrays, make_table(assign, full, count), full, count, 1),
+        over[0, 0] <= 0,
+        lambda: step(*arrays, table, *tight, count, 0),
+        lambda: step(*arrays, make_table(assign, *full, count)[0], *full, count, 1),
     )
     return (left_next[None], right_next[None], update, attended)
 

time: 109 us -> 99.1 us (0.909)
  Pallas kernels: 101 us -> 92.1 us
    pallas_call x2, Pallas kernels: 101 us -> 92.1 us  [the longest x1 90.1 us: step(): pl.pallas_call(functools.partial(step_kernel, bounds, back_cap, count), o...]
where the time goes in v5:
time: 99.1 us; the launch traced here: 98.1 us
  Pallas kernels  92.1 us (93%)
  local copies, waits for them, and re-layouts  4.5 us (5%)
  between operations  1.3 us (1%)
    pallas_call x1, Pallas kernels, step(): pl.pallas_call(functools.partial(step_kernel, bounds, back_cap, count), o...  90.1 us
    unnamed x4, local copies, waits for them, and re-layouts  4.5 us

profile of v5, /device:TPU:2, one launch (start us, length us, event | category | flops | bytes accessed | tf_op | source)
XLA Modules:
  0.0 98.1 jit_solution(1097597458213456332)
XLA Ops:
  0.6 2.0 %shard_map.102 = (s32[8,512]{1,0:T(8,128)S(1)}, s32[1,1]{1,0:T(1,128)}) custom-call(s32[1,224]{1,0:T(1,128)} %bitcast.16), custom_call_target="tpu_custom_call" | custom-call | tf_op jit(solution)/shard_map/pallas_call | solution.py:521
  3.3 90.3 %conditional.1 = ((f32[2,512,512]{2,1,0:T(8,128)S(1)}, f32[2,512,512]{2,1,0:T(8,128)S(1)}, bf16[224,8,512]{2,1,0:T(8,128)(2,1)S(1)}, bf16[256,128]{1,0:T(8,128)(2,1)S(1)})) conditional(s32[]{:T(128)} %bitcast.2, (s32[224]{0:T(256)}, bf16[256,128]{1,0:T(8,128)(2,1)}, bf16[256,128]{1,0:T(8,128)(2,1)}, bf16[256,128]{1,0:T(8,128)(2,1)}, ...), branch_computations={%region_0.0_spmd, %region_1.0_spmd} | conditional | bytes 65572 | solution.py:539
  3.5 90.1 %branch_1_fun.1 = (f32[2,512,512]{2,1,0:T(8,128)S(1)}, f32[2,512,512]{2,1,0:T(8,128)S(1)}, bf16[224,8,512]{2,1,0:T(8,128)(2,1)S(1)}, bf16[256,128]{1,0:T(8,128)(2,1)S(1)}) custom-call(s32[8,512]{1,0:T(8,128)S(1)} %get-tuple-element.51.table, bf16[256,128]{1,0:T(8,128)(2,1)} %get-tuple-element.52.query, bf16[256,128]{1,0:T(8,128)(2,1)} %get-tuple-element.53.key, ...), custom_call_target="tpu_custom_call" | custom-call | tf_op jit(solution)/shard_map/cond/branch_1_fun/pallas_call | solution.py:443
  93.6 1.3 %copy.23 = f32[1,2,512,512]{3,2,1,0:T(8,128)} copy(f32[1,2,512,512]{3,2,1,0:T(8,128)S(1)} %bitcast.14) | data formatting | bytes 4194304
  94.9 1.3 %copy.24 = f32[1,2,512,512]{3,2,1,0:T(8,128)} copy(f32[1,2,512,512]{3,2,1,0:T(8,128)S(1)} %bitcast.15) | data formatting | bytes 4194304
  96.2 1.2 %copy.25 = bf16[224,8,512]{2,1,0:T(8,128)(2,1)} copy(bf16[224,8,512]{2,1,0:T(8,128)(2,1)S(1)} %get-tuple-element.105) | data formatting | bytes 3670016
  97.4 0.6 copy.26

commit v6 on v5

--- a/solution.py
+++ b/solution.py
@@ -152,11 +152,8 @@
 
 def column_parts(order, body):
     width = min(256, order)
-
-    def one(part):
-        body(pl.ds(pl.multiple_of(part * width, width), width))
-
-    loop(order // width, one)
+    for part in range(order // width):
+        body(pl.ds(part * width, width))
 
 
 def excess(gram, result, first_b, second, second_b, third_b, tail_b, out):
@@ -361,6 +358,9 @@
     def send_back(part):
         hand_back(here, out_back[part], in_back[part], b_send.at[part], b_recv.at[part])
 
+    def sent_back(part):
+        wait_all(out_back[part].at[pl.ds(0, count - 1)], b_send.at[part])
+
     def open_gather(part):
         wait_all(in_back[part], b_recv.at[part])
         base = part // 2 * back_cap
@@ -393,15 +393,20 @@
     right_root(0)
     precondition(0)
     send_back(0)
+    left_root(1)
+    sent_back(0)
     send_back(1)
-    left_root(1)
     right_root(1)
     open_gather(0)
     precondition(1)
+    sent_back(1)
     send_back(2)
     forward(0)
+    open_gather(1)
+    sent_back(2)
     send_back(3)
-    for part in range(1, PARTS):
+    forward(1)
+    for part in (2, 3):
         open_gather(part)
         forward(part)
     for part in range(PARTS):
@@ -425,8 +430,7 @@
         wait_all(in_slabs[slot].at[pl.ds(0, count - 1)], a_send.at[slot])
         for side in range(2):
             stored(slot, side).wait()
-    for part in range(PARTS):
-        wait_all(out_back[part].at[pl.ds(0, count - 1)], b_send.at[part])
+    sent_back(3)
 
 
 def step(grads, stat_left, stat_right, query, key, value, table, bounds, back_cap, count, number):

time: 99.1 us -> 95.1 us (0.960)
  Pallas kernels: 92.1 us -> 87.3 us
    pallas_call x1, Pallas kernels: 90.1 us -> 85.3 us  [step(): pl.pallas_call(functools.partial(step_kernel, bounds, back_cap, count), o...]
where the time goes in v6:
time: 95.1 us; the launch traced here: 93.3 us
  Pallas kernels  87.3 us (92%)
  local copies, waits for them, and re-layouts  4.5 us (5%)
  between operations  1.3 us (1%)
    pallas_call x1, Pallas kernels, step(): pl.pallas_call(functools.partial(step_kernel, bounds, back_cap, count), o...  85.3 us
    unnamed x4, local copies, waits for them, and re-layouts  4.5 us
    pallas_call x1, Pallas kernels, make_table(): pl.pallas_call(functools.partial(table_kernel, bounds, back_cap, count),...  1.97 us

profile of v6, /device:TPU:2, one launch (start us, length us, event | category | flops | bytes accessed | tf_op | source)
XLA Modules:
  0.0 93.3 jit_solution(16771231974580868279)
XLA Ops:
  0.6 2.0 %shard_map.102 = (s32[8,512]{1,0:T(8,128)S(1)}, s32[1,1]{1,0:T(1,128)}) custom-call(s32[1,224]{1,0:T(1,128)} %bitcast.16), custom_call_target="tpu_custom_call" | custom-call | tf_op jit(solution)/shard_map/pallas_call | solution.py:525
  3.3 85.6 %conditional.1 = ((f32[2,512,512]{2,1,0:T(8,128)S(1)}, f32[2,512,512]{2,1,0:T(8,128)S(1)}, bf16[224,8,512]{2,1,0:T(8,128)(2,1)S(1)}, bf16[256,128]{1,0:T(8,128)(2,1)S(1)})) conditional(s32[]{:T(128)} %bitcast.2, (s32[224]{0:T(256)}, bf16[256,128]{1,0:T(8,128)(2,1)}, bf16[256,128]{1,0:T(8,128)(2,1)}, bf16[256,128]{1,0:T(8,128)(2,1)}, ...), branch_computations={%region_0.0_spmd, %region_1.0_spmd} | conditional | bytes 65572 | solution.py:543
  3.5 85.3 %branch_1_fun.1 = (f32[2,512,512]{2,1,0:T(8,128)S(1)}, f32[2,512,512]{2,1,0:T(8,128)S(1)}, bf16[224,8,512]{2,1,0:T(8,128)(2,1)S(1)}, bf16[256,128]{1,0:T(8,128)(2,1)S(1)}) custom-call(s32[8,512]{1,0:T(8,128)S(1)} %get-tuple-element.51.table, bf16[256,128]{1,0:T(8,128)(2,1)} %get-tuple-element.52.query, bf16[256,128]{1,0:T(8,128)(2,1)} %get-tuple-element.53.key, ...), custom_call_target="tpu_custom_call" | custom-call | tf_op jit(solution)/shard_map/cond/branch_1_fun/pallas_call | solution.py:447
  88.8 1.3 %copy.23 = f32[1,2,512,512]{3,2,1,0:T(8,128)} copy(f32[1,2,512,512]{3,2,1,0:T(8,128)S(1)} %bitcast.14) | data formatting | bytes 4194304
  90.1 1.3 %copy.24 = f32[1,2,512,512]{3,2,1,0:T(8,128)} copy(f32[1,2,512,512]{3,2,1,0:T(8,128)S(1)} %bitcast.15) | data formatting | bytes 4194304
  91.5 1.2 %copy.25 = bf16[224,8,512]{2,1,0:T(8,128)(2,1)} copy(bf16[224,8,512]{2,1,0:T(8,128)(2,1)S(1)} %get-tuple-element.105) | data formatting | bytes 3670016
  92.7 0.6 copy.26

commit v7 on v6

--- a/solution.py
+++ b/solution.py
@@ -388,8 +388,8 @@
         else:
             loads[1].wait()
             loads[2].wait()
-            left_root(0)
         finish(chunk)
+    left_root(0)
     right_root(0)
     precondition(0)
     send_back(0)

time: 95.1 us -> 94.2 us (level); the launches traced: 93.3 us -> 93.7 us
  no operation moved by 1% of the time
where the time goes in v7:
time: 94.2 us; the launch traced here: 93.7 us
  Pallas kernels  87.6 us (93%)
  local copies, waits for them, and re-layouts  4.5 us (5%)
  between operations  1.3 us (1%)
    pallas_call x1, Pallas kernels, step(): pl.pallas_call(functools.partial(step_kernel, bounds, back_cap, count), o...  85.7 us
    unnamed x4, local copies, waits for them, and re-layouts  4.5 us
    pallas_call x1, Pallas kernels, make_table(): pl.pallas_call(functools.partial(table_kernel, bounds, back_cap, count),...  1.97 us

profile of v7, /device:TPU:2, one launch (start us, length us, event | category | flops | bytes accessed | tf_op | source)
XLA Modules:
  0.0 93.7 jit_solution(3323530753202028223)
XLA Ops:
  0.6 2.0 %shard_map.102 = (s32[8,512]{1,0:T(8,128)S(1)}, s32[1,1]{1,0:T(1,128)}) custom-call(s32[1,224]{1,0:T(1,128)} %bitcast.16), custom_call_target="tpu_custom_call" | custom-call | tf_op jit(solution)/shard_map/pallas_call | solution.py:525
  3.3 85.9 %conditional.1 = ((f32[2,512,512]{2,1,0:T(8,128)S(1)}, f32[2,512,512]{2,1,0:T(8,128)S(1)}, bf16[224,8,512]{2,1,0:T(8,128)(2,1)S(1)}, bf16[256,128]{1,0:T(8,128)(2,1)S(1)})) conditional(s32[]{:T(128)} %bitcast.2, (s32[224]{0:T(256)}, bf16[256,128]{1,0:T(8,128)(2,1)}, bf16[256,128]{1,0:T(8,128)(2,1)}, bf16[256,128]{1,0:T(8,128)(2,1)}, ...), branch_computations={%region_0.0_spmd, %region_1.0_spmd} | conditional | bytes 65572 | solution.py:543
  3.5 85.7 %branch_1_fun.1 = (f32[2,512,512]{2,1,0:T(8,128)S(1)}, f32[2,512,512]{2,1,0:T(8,128)S(1)}, bf16[224,8,512]{2,1,0:T(8,128)(2,1)S(1)}, bf16[256,128]{1,0:T(8,128)(2,1)S(1)}) custom-call(s32[8,512]{1,0:T(8,128)S(1)} %get-tuple-element.51.table, bf16[256,128]{1,0:T(8,128)(2,1)} %get-tuple-element.52.query, bf16[256,128]{1,0:T(8,128)(2,1)} %get-tuple-element.53.key, ...), custom_call_target="tpu_custom_call" | custom-call | tf_op jit(solution)/shard_map/cond/branch_1_fun/pallas_call | solution.py:447
  89.2 1.3 %copy.23 = f32[1,2,512,512]{3,2,1,0:T(8,128)} copy(f32[1,2,512,512]{3,2,1,0:T(8,128)S(1)} %bitcast.14) | data formatting | bytes 4194304
  90.5 1.3 %copy.24 = f32[1,2,512,512]{3,2,1,0:T(8,128)} copy(f32[1,2,512,512]{3,2,1,0:T(8,128)S(1)} %bitcast.15) | data formatting | bytes 4194304
  91.8 1.2 %copy.25 = bf16[224,8,512]{2,1,0:T(8,128)(2,1)} copy(bf16[224,8,512]{2,1,0:T(8,128)(2,1)S(1)} %get-tuple-element.105) | data formatting | bytes 3670016
  93.0 0.6 copy.26
